TPU v7x, 512 devices: a whole 4x4x16 slice. The times are simulated.
512 devices in a mesh: row: 16 (over z), col: 32 (over x, y, core).
Axes of the slice: x: 4, y: 4, z: 16, core: 2. Of those that a mesh axis runs over, the one named last changes fastest.
Arguments:
- jacobians: bfloat16 [1024, 60, 190], P(('row', 'col')), may hold values from -0.4375 to 0.4375
- descriptors: bfloat16 [1024, 190], P(('row', 'col')), may hold values from -6 to 6
- block_inverse: bfloat16 [960, 960], replicated
- tile_order: int32 [1024], replicated, may hold values from 0 to 1023, each once
- panel: int32 [1], replicated, may hold values from 0 to 62
Outputs:
- panel_factor: bfloat16 [61440, 960], P(('row', 'col'))
- next_column: bfloat16 [61440, 960], P(('row', 'col'))
Inputs may be any that keep to these rules, and one draw needn't show every extreme that they name: `tile_order`: each conformer once. The next panel exists.
All inputs are finite; a program needn't handle non-finite values.
Results may differ from a plain program's by a relative error of at most 0.0051.
Values may be sent and summed in bfloat16 or wider, within the bound.
A program may use at most 64 MiB of HBM per device.

v0:
```python
import math

import jax
import jax.numpy as jnp
from jax import lax
from jax.sharding import PartitionSpec as P


def kernel_block(jac_rows, desc_rows, jac_cols, desc_cols):
    count_a, ncomp, ndesc = jac_rows.shape
    count_b = jac_cols.shape[0]
    width = 2.0 * math.sqrt(2.0 * ndesc)
    inner = lax.dot_general(
        jac_rows.reshape(count_a * ncomp, ndesc),
        jac_cols.reshape(count_b * ncomp, ndesc),
        (((1,), (1,)), ((), ())),
        preferred_element_type=jnp.float32,
    )
    inner = inner.reshape(count_a, ncomp, count_b, ncomp)
    diff = desc_rows.astype(jnp.float32)[:, None, :] - desc_cols.astype(jnp.float32)[None, :, :]
    dist = jnp.sqrt(jnp.sum(diff * diff, axis=-1))
    scaled = math.sqrt(5.0) * dist / width
    decay = jnp.exp(-scaled)
    left = jnp.einsum(
        "abd,acd->abc", diff, jac_rows.astype(jnp.float32), precision=lax.Precision.HIGHEST
    )
    right = jnp.einsum(
        "abd,bed->abe", diff, jac_cols.astype(jnp.float32), precision=lax.Precision.HIGHEST
    )
    outer = jnp.einsum("abc,abe->acbe", left, right, precision=lax.Precision.HIGHEST)
    first = (decay * (1.0 + scaled))[:, None, :, None]
    second = (decay * (5.0 / (width * width)))[:, None, :, None]
    kern = first * inner - second * outer
    return kern.reshape(count_a * ncomp, count_b * ncomp)


def masked_terms(wanted, offset, jacobians, descriptors):
    rows = jacobians.shape[0]
    owned = offset + jnp.arange(rows, dtype=jnp.int32)
    select = (wanted[:, None] == owned[None, :]).astype(jnp.bfloat16)
    picked_jac = jnp.dot(select, jacobians.reshape(rows, -1), preferred_element_type=jnp.float32)
    picked_desc = jnp.dot(select, descriptors, preferred_element_type=jnp.float32)
    return (picked_jac, picked_desc)


def shards(jacobians, descriptors, block_inverse, tile_order, panel):
    rows, ncomp, ndesc = jacobians.shape
    pcols = block_inverse.shape[0]
    count = pcols // ncomp
    offset = (lax.axis_index("row") * lax.axis_size("col") + lax.axis_index("col")) * rows
    start = panel[0] * count
    ids_panel = lax.dynamic_slice(tile_order, (start,), (count,))
    ids_next = lax.dynamic_slice(tile_order, (start + count,), (count,))
    wanted = jnp.concatenate([ids_panel, ids_next], axis=0)
    both_terms = masked_terms(wanted, offset, jacobians, descriptors)
    both_sums = lax.psum((both_terms[0], both_terms[1]), ("row", "col"))
    jac_both = both_sums[0].astype(jnp.bfloat16).reshape(2 * count, ncomp, ndesc)
    desc_both = both_sums[1].astype(jnp.bfloat16)
    jac_panel = jac_both[:count]
    jac_next = jac_both[count:]
    desc_panel = desc_both[:count]
    desc_next = desc_both[count:]
    tiles = kernel_block(jacobians, descriptors, jac_panel, desc_panel).astype(jnp.bfloat16)
    factor = lax.dot_general(
        tiles, block_inverse, (((1,), (1,)), ((), ())), preferred_element_type=jnp.float32
    ).astype(jnp.bfloat16)
    fresh = kernel_block(jacobians, descriptors, jac_next, desc_next)
    share = count // lax.axis_size("row")
    first = lax.axis_index("row") * share
    jac_share = lax.dynamic_slice_in_dim(jac_next, first, share, 0)
    desc_share = lax.dynamic_slice_in_dim(desc_next, first, share, 0)
    cross_share = kernel_block(jac_panel, desc_panel, jac_share, desc_share).astype(jnp.bfloat16)
    solved_share = jnp.dot(block_inverse, cross_share, preferred_element_type=jnp.float32).astype(
        jnp.bfloat16
    )
    correction = jnp.dot(
        factor,
        lax.all_gather(solved_share, "row", axis=1, tiled=True),
        preferred_element_type=jnp.float32,
    )
    updated = (fresh - correction).astype(jnp.bfloat16)
    return (factor, updated)


def solution(mesh):
    placed = (P(("row", "col"), None, None), P(("row", "col"), None), P(), P(), P())
    return jax.shard_map(
        shards,
        mesh=mesh,
        in_specs=placed,
        out_specs=(P(("row", "col"), None), P(("row", "col"), None)),
        check_vma=False,
    )
```

profile of v0, /device:TPU:4, one launch (start us, length us, event | category | flops | bytes accessed | tf_op | source)
XLA Modules:
  0.0 222.3 jit_solution(5172691623062593210)
XLA Ops:
  7.2 0.0 copy-start
  7.2 0.0 all-gather.3.cloned.1.call-start
  8.0 0.8 copy.29
  8.9 0.0 copy-start.4
  8.9 0.2 reshape.121
  9.1 0.8 fusion.43
  10.0 0.0 copy-done.4
  10.0 0.1 pad_add_fusion
  10.1 0.4 fusion.16
  10.5 0.9 fusion.18
  11.3 115.6 %all-reduce.2 = (bf16[32,11400]{1,0:T(8,128)(2,1)}, bf16[32,190]{1,0:T(8,128)(2,1)S(1)}) all-reduce(f32[32,11400]{1,0:T(8,128)S(1)} %fusion.16, f32[32,190]{1,0:T(8,128)S(1)} %fusion.18), channel_id=1, replica_groups=mesh['row'=16,'col'=32] {'row','col'}, use_global_device_ids=true, to_apply=%region_2.0 | all-reduce | flops 370880 | bytes 2225280 | tf_op jit(solution)/shard_map/psum | solution.py:56
  127.0 1.1 fusion.41
  128.1 0.6 fusion.42
  128.7 2.3 %slice.20 = bf16[16,60,190]{2,1,0:T(8,128)(2,1)} reshape(bf16[16,11400]{1,0:T(8,128)(2,1)S(1)} %get-tuple-element.7) | data formatting | bytes 729600 | tf_op jit(solution)/shard_map/slice | solution.py:59
  131.0 1.5 slice.23
  132.5 0.1 multiply_reduce_fusion.2
  132.6 0.1 convolution_bitcast_fusion.4
  132.8 1.6 fusion.20
  134.3 2.1 fusion.2
  136.4 1.0 reshape.137
  137.4 0.0 copy-done
  137.4 1.4 fusion.4
  138.8 0.0 all-gather.3.cloned.1.call-update
  138.8 1.5 reshape.122
  140.3 0.0 copy-start.3
  140.3 0.9 reshape.123
  141.2 0.0 copy-start.5
  141.2 0.7 convert_element_type.49
  141.9 1.5 reshape.125
  143.5 0.0 copy-done.5
  143.5 2.1 convolution_bitcast_fusion.1
  145.6 1.6 reshape.124
  147.2 0.0 copy-done.3
  147.2 0.9 fusion.12
  148.1 0.6 copy.35
  148.7 1.9 multiply_reduce_fusion
  150.7 2.2 convolution_bitcast_fusion.3
  152.9 1.8 copy.33
  154.6 1.3 add_multiply_fusion
  155.9 1.4 copy.31
  157.3 1.3 copy.28
  158.6 2.9 %fusion.5 = bf16[2,60,16,60]{1,0,3,2:T(2,128)(2,1)} fusion(f32[2,60,16,60]{1,0,3,2:T(2,128)S(1)} %reshape.124, f32[2,16,60]{2,0,1:T(2,128)} %copy.35, f32[2,16,60]{0,2,1:T(8,128)} %copy.33, f32[2,16]{0,1:T(8,128)} %copy.31, f32[2,16]{0,1:T(8,128)} %copy.28), kind=kLoop, calls=%fused_computation.16 | loop fusion | flops 576000 | bytes 706816 | tf_op jit(solution)/shard_map/convert_element_type | solution.py:63
  161.5 2.0 convert_element_type.54
  163.5 2.1 convolution_bitcast_fusion
  165.6 1.6 reshape.126
  167.2 0.1 fusion.10
  167.4 1.3 convolution_bitcast_fusion.2
  168.6 0.3 copy.39
  168.9 0.7 copy.37
  169.7 0.7 copy.36
  170.3 2.0 bitcast_subtract_fusion
  172.3 0.0 copy-start.1
  172.3 1.8 reshape.136
  174.2 0.2 copy.46
  174.4 0.0 copy-done.1
  174.4 0.7 convolution_convert_fusion
  175.1 0.0 copy-start.2
  175.1 33.4 %all-gather.3.cloned.1.call-done = bf16[16,60,960]{2,1,0:T(8,128)(2,1)} async-done(((bf16[1,60,960]{2,1,0:T(8,128)(2,1)}), bf16[16,60,960]{2,1,0:T(8,128)(2,1)}) %all-gather.3.cloned.1.call-update) | async-done | bytes 1843216 | tf_op jit(solution)/shard_map/all_gather | solution.py:78
  208.5 4.0 %reshape.132 = bf16[960,960]{1,0:T(8,128)(2,1)} reshape(bf16[16,60,960]{2,1,0:T(8,128)(2,1)} %all-gather.3.cloned.1.call-done) | data formatting | bytes 3686400
  212.4 0.0 copy-done.2
  212.4 3.0 %fusion.3 = bf16[120,960]{1,0:T(8,128)(2,1)} fusion(f32[120,960]{1,0:T(8,128)S(1)} %copy.46, bf16[120,960]{1,0:T(8,128)(2,1)S(1)} %convolution_convert_fusion, bf16[960,960]{1,0:T(8,128)(2,1)} %reshape.132), kind=kOutput, calls=%fused_computation.7 | convolution fusion | flops 221414400 | bytes 2764800 | tf_op jit(solution)/shard_map/dot_general | solution.py:76
  (4 shorter events, 0.1 us)
Async XLA Ops:
  7.2 130.3 %copy-start = (bf16[960,960]{1,0:T(8,128)(2,1)S(1)}, bf16[960,960]{1,0:T(8,128)(2,1)}, u32[]{:S(2)}) copy-start(bf16[960,960]{1,0:T(8,128)(2,1)} %param.7) | copy-start | bytes 5529604
  7.2 201.3 %all-gather.3.cloned.1.call-start = ((), (), s32[]{:S(2)}) async-start(), calls=%async_computation | async-start | bytes 2228224 | tf_op jit(solution)/shard_map/all_gather | solution.py:78
  8.9 1.1 copy-start.4
  140.3 6.9 %copy-start.3 = (bf16[2,60,190]{2,0,1:T(2,128)(2,1)S(1)}, bf16[2,60,190]{2,0,1:T(2,128)(2,1)}, u32[]{:S(2)}) copy-start(bf16[2,60,190]{2,0,1:T(2,128)(2,1)} %param.5) | copy-start | bytes 136804
  141.2 2.3 %copy-start.5 = (bf16[120,190]{1,0:T(8,128)(2,1)}, bf16[120,190]{1,0:T(8,128)(2,1)S(1)}, u32[]{:S(2)}) copy-start(bf16[120,190]{1,0:T(8,128)(2,1)S(1)} %reshape.123) | copy-start | bytes 136804
  172.3 2.0 copy-start.1
  175.1 37.3 %copy-start.2 = (bf16[120,960]{1,0:T(8,128)(2,1)}, bf16[120,960]{1,0:T(8,128)(2,1)S(1)}, u32[]{:S(2)}) copy-start(bf16[120,960]{1,0:T(8,128)(2,1)S(1)} %convolution_convert_fusion) | copy-start | bytes 691204
Sparse Core Ops, SparseCore 0:
  138.9 69.4 all-gather.2
where the time goes:
time: 223 us; the launch traced here: 222 us
  blocking collectives  116 us (52%)
  waiting for transfers between devices  33.4 us (15%)
  local copies, waits for them, and re-layouts  29.8 us (13%)
  matrix products  18.8 us (8%)
  between operations  15 us (7%)
  other arithmetic  9.65 us (4%)
    psum x1, blocking collectives, shards(): both_sums = lax.psum((both_terms[0], both_terms[1]), ('row', 'col'))  116 us
    all_gather x1, waiting for transfers between devices, shards(): lax.all_gather(solved_share, 'row', axis=1, tiled=True)  33.4 us
    dot_general x3, matrix products, kernel_block(): lax.dot_general(jac_rows.reshape(count_a * ncomp, ndesc), jac_cols.reshap...  6.3 us
    unnamed x14, local copies, waits for them, and re-layouts  4.83 us
  transfers between devices with their start and end apart: 1, of which 1 were waited for; matrix products, arithmetic and copies ran while one was open for 16% of the time, Pallas kernels for 0%

commit v1 on v0

v1 whole, which is shorter than its diff:
```python
import functools
import math

import jax
import jax.numpy as jnp
from jax import lax
from jax.experimental import pallas as pl
from jax.experimental.pallas import tpu as pltpu
from jax.sharding import PartitionSpec as P

MESH = pl.DeviceIdType.MESH
F32 = jnp.float32
BF16 = jnp.bfloat16
NC = 60
ND = 190
PB = 64
TR = 16
TL = 128
NZ = 16
NCH = 16
SLOTS = 32
CHUNKS = 12

NT = (((1,), (1,)), ((), ()))
NN = (((1,), (0,)), ((), ()))


def dot(a, b, dims):
    return lax.dot_general(a, b, dims, preferred_element_type=F32)


def own_blocks(jac_ref, desc_ref, blk, send1):
    blk[...] = jnp.zeros_like(blk)
    for i in range(2):
        jac = jac_ref[i]
        desc = desc_ref[i : i + 1, :]
        jac32 = jac.astype(F32)
        desc32 = desc.astype(F32)
        col = jnp.sum(jac32 * desc32, axis=1, keepdims=True)
        high = col.astype(BF16).astype(F32)
        row = dot(jnp.broadcast_to(desc32, (8, ND)).astype(BF16), jac, NT)[0:1, :]
        row_high = row.astype(BF16).astype(F32)
        blk[i, 0:NC, 0:ND] = jac32
        blk[i, 0:NC, ND : ND + 1] = high
        blk[i, 0:NC, ND + 1 : ND + 2] = col - high
        blk[i, NC : NC + 1, 0:ND] = desc32
        blk[i, NC + 1 : NC + 2, 0:NC] = row_high
        blk[i, NC + 1 : NC + 2, PB : PB + NC] = row_high
        blk[i, NC + 2 : NC + 3, 0:NC] = row - row_high
        blk[i, NC + 2 : NC + 3, PB : PB + NC] = row - row_high
    lane = lax.broadcasted_iota(jnp.int32, (TR, TL), 1)
    for r in range(4):
        rows = slice(TR * r, TR * r + TR)
        send1[2 * r] = blk[0, rows, 0:TL].astype(BF16)
        send1[2 * r + 1] = blk[1, rows, 0:TL].astype(BF16)
        first = blk[0, rows, TL : 2 * TL]
        second = pltpu.roll(blk[1, rows, TL : 2 * TL], 64, 1)
        send1[8 + r] = jnp.where(lane < 64, first, second).astype(BF16)


def exchange(
    order_ref, panel_ref, jac_ref, desc_ref, own_ref, all_ref,
    blk, got1, send2, got2, mine, s1, r1, s2, r2, s3, r3, s4, r4, s5, r5,
):
    z = lax.axis_index("row")
    col = lax.axis_index("col")
    core = col % 2
    chip = col // 2
    sib = chip * 2 + 1 - core

    barrier = pltpu.get_barrier_semaphore()
    for d in range(1, NZ):
        pl.semaphore_signal(barrier, inc=1, device_id=((z + d) % NZ, col), device_id_type=MESH)
    for d in range(1, 2 * NCH):
        pl.semaphore_signal(barrier, inc=1, device_id=(z, (col + d) % (2 * NCH)), device_id_type=MESH)
    own_blocks(jac_ref, desc_ref, blk, own_ref)
    pl.semaphore_wait(barrier, NZ - 1 + 2 * NCH - 1)

    holds = z < CHUNKS
    is_y = jnp.logical_and(z >= 4, z < 8)
    is_x = jnp.logical_and(holds, jnp.logical_or(z < 4, z >= 8))

    def part(k):
        return (2 * (k % 4), 2) if k < 4 or k >= 8 else (8 + k % 4, 1)

    for k in range(CHUNKS):
        first, n = part(k)

        def send(k=k, first=first, n=n):
            pltpu.make_async_remote_copy(
                own_ref.at[pl.ds(first, n)], got1.at[z, pl.ds(0, n)], s1, r1,
                device_id=(k, col), device_id_type=MESH,
            ).start()

        def keep(k=k, first=first, n=n):
            got1[k, 0:n] = own_ref[first : first + n]

        pl.when(z != k)(send)
        pl.when(z == k)(keep)

    def slot(s):
        conf = order_ref[panel_ref[0] * (SLOTS // 2) + s]
        return conf // (4 * NCH), (conf // 2) % (2 * NCH) == col, conf % 2

    zeros = jnp.zeros((TR, TL), F32)

    @pl.when(is_x)
    def _():
        pltpu.make_async_copy(got1.at[0 : NZ - 1], got1.at[0 : NZ - 1], r1).wait()

    @pl.when(is_y)
    def _():
        pltpu.make_async_copy(send2.at[0 : NZ - 1], send2.at[0 : NZ - 1], r1).wait()

    for odd in range(2):

        @pl.when(jnp.logical_and(is_x, (z >= 8) == (odd == 1)))
        def _(odd=odd):
            for j in range(NCH):
                where, hit, i = slot(2 * j + odd)
                tile = got1[where, i].astype(F32)
                send2[j] = jnp.where(hit, tile, zeros).astype(BF16)

    @pl.when(is_y)
    def _():
        lane = lax.broadcasted_iota(jnp.int32, (TR, TL), 1)
        for j in range(NCH):
            where0, hit0, i0 = slot(2 * j)
            where1, hit1, i1 = slot(2 * j + 1)
            t0 = got1[where0, 0].astype(F32)
            t1 = got1[where1, 0].astype(F32)
            t0 = jnp.where(i0 == 0, t0, pltpu.roll(t0, 64, 1))
            t1 = jnp.where(i1 == 1, t1, pltpu.roll(t1, 64, 1))
            t0 = jnp.where(hit0, t0, zeros)
            t1 = jnp.where(hit1, t1, zeros)
            send2[j] = jnp.where(lane < 64, t0, t1).astype(BF16)

    turn = z % 2

    @pl.when(holds)
    def _():
        for j in range(NCH):
            to = 2 * j + turn

            @pl.when(to != col)
            def _(j=j, to=to):
                pltpu.make_async_remote_copy(
                    send2.at[j], got2.at[(col + 2 * NCH - to) % (2 * NCH)], s2, r2,
                    device_id=(z, to), device_id_type=MESH,
                ).start()

            @pl.when(to == col)
            def _(j=j):
                got2[0] = send2[j]

    reduces = jnp.logical_and(holds, core == turn)
    place = z // 2

    @pl.when(reduces)
    def _():
        pltpu.make_async_copy(got2.at[1 : 2 * NCH], got2.at[1 : 2 * NCH], r2).wait()
        total = got2[0].astype(F32)
        for n in range(1, 2 * NCH):
            total = total + got2[n].astype(F32)
        mine[place] = total.astype(BF16)
        for d in range(1, NZ):
            pltpu.make_async_remote_copy(
                mine.at[place], mine.at[place], s3, r3,
                device_id=((z + d) % NZ, col), device_id_type=MESH,
            ).start()
        pltpu.make_async_copy(mine.at[0:5], mine.at[0:5], r3).wait()

    @pl.when(jnp.logical_not(reduces))
    def _():
        pltpu.make_async_copy(mine.at[0:6], mine.at[0:6], r3).wait()

    all_ref[core, chip] = mine[...]
    x, y = chip // 4, chip % 4
    steps = [(dx, dy) for dx in range(4) for dy in range(4) if dx or dy]
    steps.sort(key=lambda d: min(d[0], 4 - d[0]) + min(d[1], 4 - d[1]), reverse=True)
    for n, (dx, dy) in enumerate(steps):
        to = (((x + dx) % 4) * 4 + (y + dy) % 4) * 2 + core
        pltpu.make_async_remote_copy(
            mine, all_ref.at[core, chip], s4, r4.at[n], device_id=(z, to), device_id_type=MESH
        ).start()
    pltpu.make_async_remote_copy(
        mine, all_ref.at[core, chip], s5, r5, device_id=(z, sib), device_id_type=MESH
    ).start()
    for n, (dx, dy) in reversed(list(enumerate(steps))):
        source = ((x + 4 - dx) % 4) * 4 + (y + 4 - dy) % 4
        landed = all_ref.at[core, source]
        pltpu.make_async_copy(landed, landed, r4.at[n]).wait()
        pltpu.make_async_remote_copy(
            landed, landed, s5, r5, device_id=(z, sib), device_id_type=MESH
        ).start()
    other = all_ref.at[1 - core]
    pltpu.make_async_copy(other, other, r5).wait()

    pltpu.make_async_copy(other, other, s5).wait()
    pltpu.make_async_copy(all_ref.at[0, 0:15], all_ref.at[0, 0:15], s4).wait()

    @pl.when(reduces)
    def _():
        pltpu.make_async_copy(got2.at[0 : NZ - 1], got2.at[0 : NZ - 1], s3).wait()

    @pl.when(reduces)
    def _():
        pltpu.make_async_copy(got2.at[0 : NCH - 1], got2.at[0 : NCH - 1], s2).wait()

    @pl.when(jnp.logical_and(holds, core != turn))
    def _():
        pltpu.make_async_copy(got2.at[0:NCH], got2.at[0:NCH], s2).wait()

    @pl.when(is_x)
    def _():
        pltpu.make_async_copy(got2.at[0:18], got2.at[0:18], s1).wait()

    @pl.when(is_y)
    def _():
        pltpu.make_async_copy(got2.at[0:19], got2.at[0:19], s1).wait()

    @pl.when(jnp.logical_not(holds))
    def _():
        pltpu.make_async_copy(got2.at[0:20], got2.at[0:20], s1).wait()


def compute(own_ref, all_ref, inv_ref, factor_ref, next_ref, rhs, dexp, lhs, f1s, qqs, cross, solved, inv, outs):
    width = 2.0 * math.sqrt(2.0 * ND)
    lane = lax.broadcasted_iota(jnp.int32, (TR, TL), 1)
    low = lane < 64
    ones_lane = jnp.logical_and(lane >= 62, lane < 64)
    pad = NCH * PB

    rows_i = lax.broadcasted_iota(jnp.int32, (NCH * NC, pad), 0)
    cols_i = lax.broadcasted_iota(jnp.int32, (NCH * NC, pad), 1)
    block = cols_i // PB
    spread = jnp.where(
        jnp.logical_and(rows_i - block * NC == cols_i - block * PB, cols_i - block * PB < NC), 1.0, 0.0
    ).astype(BF16)
    inv[...] = dot(inv_ref[...], spread, NN).astype(BF16)

    def tile(j, kind, r):
        return all_ref[r % 2, j, kind * 2 + r // 2].astype(F32)

    def canon(y, odd):
        turned = pltpu.roll(y, 64, 1)
        return jnp.where(low, turned, y) if odd else jnp.where(low, y, turned)

    descs = []
    srows = []
    for j in range(NCH):
        sums = []
        for odd in range(2):
            base = TL * j + PB * odd
            for r in range(4):
                xt = tile(j, 2 if odd else 0, r)
                yt = tile(j, 1, r)
                keep = jnp.logical_and(lane >= 64, lane < 126) if odd else lane < 62
                rows = slice(base + TR * r, base + TR * r + TR)
                rhs[rows, 0:TL] = xt.astype(BF16)
                rhs[rows, TL : 2 * TL] = jnp.where(keep, yt, 0.0).astype(BF16)
                if j < NCH // 2:
                    lhs[rows, 0:TL] = xt.astype(BF16)
                    lhs[rows, TL : 2 * TL] = canon(yt, odd).astype(BF16)
                if r == 3:
                    d0 = xt[12:13, :]
                    d1 = canon(yt, odd)[12:13, :]
                    sums.append(xt[13:14, :] + xt[14:15, :])
                    descs.append((d0, d1))
            e0 = jnp.broadcast_to(d0, (TR, TL)).astype(BF16)
            e1 = jnp.broadcast_to(d1, (TR, TL))
            e1 = jnp.where(ones_lane, -1.0, jnp.where(low, e1, 0.0)).astype(BF16)
            for r in range(4):
                rows = slice(base + TR * r, base + TR * r + TR)
                dexp[rows, 0:TL] = e0
                dexp[rows, TL : 2 * TL] = e1
        srows.append(jnp.where(low[0:1], sums[0], sums[1]))
    srow = jnp.concatenate(srows, axis=1)

    for i in range(2):
        for r in range(4):
            rows = slice(NCH * PB + PB * i + TR * r, NCH * PB + PB * i + TR * r + TR)
            yt = canon(own_ref[8 + r].astype(F32), i)
            lhs[rows, 0:TL] = own_ref[2 * r + i]
            lhs[rows, TL : 2 * TL] = yt.astype(BF16)
            if r == 3:
                descs.append((own_ref[2 * r + i].astype(F32)[12:13, :], yt[12:13, :]))

    pick = list(range(NCH)) + [SLOTS, SLOTS + 1]
    zero_row = jnp.zeros((1, TL), F32)
    d0s = jnp.concatenate([descs[p][0] for p in pick] + [zero_row] * 6, axis=0)
    d1s = jnp.concatenate([descs[p][1] for p in pick] + [zero_row] * 6, axis=0)
    drows = jnp.concatenate([d0s, d1s], axis=1).astype(BF16)
    q = dot(drows, rhs[...], NT) - srow
    half = jnp.where(lax.broadcasted_iota(jnp.int32, (24, TL), 1) < 64, 1.0, 0.0)
    dists = []
    for j in range(NCH):
        cols = []
        for odd in range(2):
            u0 = d0s - descs[2 * j + odd][0]
            u1 = (d1s - descs[2 * j + odd][1]) * half
            cols.append(jnp.sum(u0 * u0 + u1 * u1, axis=1, keepdims=True))
        dists.append(jnp.where(half > 0.5, cols[0], cols[1]))
    dist = jnp.sqrt(jnp.concatenate(dists, axis=1))
    scaled = (math.sqrt(5.0) / width) * dist
    decay = jnp.exp(-scaled)
    f1s[...] = decay * (1.0 + scaled)
    qqs[...] = decay * (5.0 / (width * width)) * q

    own_lhs = lhs[pad : pad + TL, :]
    prod = dot(own_lhs, rhs[...], NT)
    prod2 = dot(own_lhs, dexp[...], NT)
    upper = lax.broadcasted_iota(jnp.int32, (TL, 1), 0) < PB
    f1 = jnp.where(upper, f1s[16:17, :], f1s[17:18, :])
    qq = jnp.where(upper, qqs[16:17, :], qqs[17:18, :])
    tiles = prod * f1 + prod2 * qq
    fresh = tiles[:, pad:]
    factor = dot(tiles[:, 0:pad].astype(BF16), inv[...], NT)
    outs[0:NC, :] = factor[0:NC, :]
    outs[NC : 2 * NC, :] = factor[PB : PB + NC, :]
    factor_ref[...] = outs[...].astype(BF16)

    @pl.loop(0, 4)
    def _(g):
        rows = pl.ds(pl.multiple_of(g * 256, 256), 256)
        part = lhs[rows, :]
        a = dot(part, rhs[pad:, :], NT)
        b = dot(part, dexp[pad:, :], NT)
        for i in range(4):
            f1_row = f1s[pl.ds(g * 4 + i, 1), pad:]
            qq_row = qqs[pl.ds(g * 4 + i, 1), pad:]
            got = a[PB * i : PB * i + PB, :] * f1_row + b[PB * i : PB * i + PB, :] * qq_row
            cross[pl.ds(pl.multiple_of(g * 256 + PB * i, PB), PB), :] = got.astype(BF16)

    @pl.loop(0, 3)
    def _(g):
        rows = pl.ds(pl.multiple_of(g * 320, 320), 320)
        solved[rows, :] = dot(inv[rows, :], cross[...], NN).astype(BF16)

    updated = (fresh - dot(factor.astype(BF16), solved[...], NN)).astype(BF16)
    final = dot(updated, spread, NT)
    outs[0:NC, :] = final[0:NC, :]
    outs[NC : 2 * NC, :] = final[PB : PB + NC, :]
    next_ref[...] = outs[...].astype(BF16)


VM = pl.BlockSpec(memory_space=pltpu.VMEM)
SM = pl.BlockSpec(memory_space=pltpu.SMEM)


def shards(jacobians, descriptors, block_inverse, tile_order, panel):
    own, everything = pl.pallas_call(
        exchange,
        name="exchange",
        out_shape=(
            jax.ShapeDtypeStruct((CHUNKS, TR, TL), BF16),
            jax.ShapeDtypeStruct((2, NCH, CHUNKS // 2, TR, TL), BF16),
        ),
        in_specs=[SM, SM, VM, VM],
        out_specs=(VM, VM),
        scratch_shapes=[
            pltpu.VMEM((2, PB, 2 * TL), F32),
            pltpu.VMEM((NZ, 2, TR, TL), BF16),
            pltpu.VMEM((NCH, TR, TL), BF16),
            pltpu.VMEM((2 * NCH, TR, TL), BF16),
            pltpu.VMEM((CHUNKS // 2, TR, TL), BF16),
            pltpu.SemaphoreType.DMA,
            pltpu.SemaphoreType.DMA,
            pltpu.SemaphoreType.DMA,
            pltpu.SemaphoreType.DMA,
            pltpu.SemaphoreType.DMA,
            pltpu.SemaphoreType.DMA,
            pltpu.SemaphoreType.DMA,
            pltpu.SemaphoreType.DMA((NCH - 1,)),
            pltpu.SemaphoreType.DMA,
            pltpu.SemaphoreType.DMA,
        ],
        compiler_params=pltpu.CompilerParams(
            collective_id=0, has_side_effects=True, vmem_limit_bytes=16 * 2**20
        ),
    )(tile_order, panel, jacobians, descriptors)
    pad = NCH * PB
    rows, pcols = jacobians.shape[0] * NC, block_inverse.shape[0]
    return pl.pallas_call(
        compute,
        name="compute",
        out_shape=(jax.ShapeDtypeStruct((rows, pcols), BF16),) * 2,
        in_specs=[VM, VM, VM],
        out_specs=(VM, VM),
        scratch_shapes=[
            pltpu.VMEM((2 * pad, 2 * TL), BF16),
            pltpu.VMEM((2 * pad, 2 * TL), BF16),
            pltpu.VMEM((pad + TL, 2 * TL), BF16),
            pltpu.VMEM((24, 2 * pad), F32),
            pltpu.VMEM((24, 2 * pad), F32),
            pltpu.VMEM((pad, pad), BF16),
            pltpu.VMEM((pcols, pad), BF16),
            pltpu.VMEM((pcols, pad), BF16),
            pltpu.VMEM((rows, pcols), F32),
        ],
        compiler_params=pltpu.CompilerParams(vmem_limit_bytes=48 * 2**20),
    )(own, everything, block_inverse)


def solution(mesh):
    placed = (P(("row", "col"), None, None), P(("row", "col"), None), P(), P(), P())
    return jax.shard_map(
        shards,
        mesh=mesh,
        in_specs=placed,
        out_specs=(P(("row", "col"), None), P(("row", "col"), None)),
        check_vma=False,
    )
```

time: 223 us -> 62.4 us (0.28)
  the two profiles are of different devices: /device:TPU:4 before, /device:TPU:1 now
where the time goes in v1:
time: 62.4 us; the launch traced here: 62.1 us
  Pallas kernels  57.1 us (92%)
  local copies, waits for them, and re-layouts  3.74 us (6%)
  between operations  1.31 us (2%)
    pallas_call x1, Pallas kernels, shards(): pl.pallas_call(exchange, name='exchange', out_shape=(jax.ShapeDtypeStruct...  46.9 us
    pallas_call x1, Pallas kernels, shards(): pl.pallas_call(compute, name='compute', out_shape=(jax.ShapeDtypeStruct((...  10.2 us
    unnamed x7, local copies, waits for them, and re-layouts  3.74 us

profile of v1, /device:TPU:1, one launch (start us, length us, event | category | flops | bytes accessed | tf_op | source)
XLA Modules:
  0.0 62.1 jit_solution(6909225027512605048)
XLA Ops:
  1.3 0.8 %copy.7.jac_ref = bf16[2,60,190]{2,1,0:T(8,128)(2,1)S(1)} copy(bf16[2,60,190]{2,0,1:T(2,128)(2,1)} %param.5) | data formatting | bytes 91200 | tf_op args[0]
  2.1 0.0 copy-start.1
  2.1 0.7 %copy-done.1 = s32[1024]{0:T(1024)S(1)} copy-done((s32[1024]{0:T(1024)S(1)}, s32[1024]{0:T(1024)}, u32[]{:S(2)}) %copy-start.1) | copy-done | bytes 4120
  2.8 0.0 copy-start.2
  2.8 0.7 %copy-done.2 = bf16[2,190]{1,0:T(2,128)(2,1)S(1)} copy-done((bf16[2,190]{1,0:T(2,128)(2,1)S(1)}, bf16[2,190]{1,0:T(2,128)(2,1)}, u32[]{:S(2)}) %copy-start.2) | copy-done | bytes 784
  3.5 46.9 %exchange.1 = (bf16[12,16,128]{2,1,0:T(8,128)(2,1)S(1)}, bf16[2,16,6,16,128]{4,3,2,1,0:T(8,128)(2,1)S(1)}) custom-call(s32[1024]{0:T(1024)S(1)} %copy-done.1, s32[1]{0:T(128)S(6)} %copy.8.panel_ref, bf16[2,60,190]{2,1,0:T(8,128)(2,1)S(1)} %copy.7.jac_ref, bf16[2,190]{1,0:T(2,128)(2,1)S(1)} %copy-done.2), custom_call_target="tpu_custom_call" | custom-call | tf_op jit(solution)/shard_map/exchange/pallas_call | solution.py:352
  50.4 0.0 copy-start
  50.4 1.5 %copy-done = bf16[960,960]{1,0:T(8,128)(2,1)S(1)} copy-done((bf16[960,960]{1,0:T(8,128)(2,1)S(1)}, bf16[960,960]{1,0:T(8,128)(2,1)}, u32[]{:S(2)}) %copy-start) | copy-done | bytes 1843224
  51.9 10.2 %compute.1 = (bf16[120,960]{1,0:T(8,128)(2,1)}, bf16[120,960]{1,0:T(8,128)(2,1)}) custom-call(bf16[12,16,128]{2,1,0:T(8,128)(2,1)S(1)} %get-tuple-element.4.own_ref, bf16[2,16,6,16,128]{4,3,2,1,0:T(8,128)(2,1)S(1)} %get-tuple-element.5.all_ref, bf16[960,960]{1,0:T(8,128)(2,1)S(1)} %copy-done), custom_call_target="tpu_custom_call" | custom-call | tf_op jit(solution)/shard_map/compute/pallas_call | solution.py:384
Async XLA Ops:
  2.1 0.7 %copy-start.1 = (s32[1024]{0:T(1024)S(1)}, s32[1024]{0:T(1024)}, u32[]{:S(2)}) copy-start(s32[1024]{0:T(1024)} %order_ref.1) | copy-start | bytes 12292
  2.8 0.7 %copy-start.2 = (bf16[2,190]{1,0:T(2,128)(2,1)S(1)}, bf16[2,190]{1,0:T(2,128)(2,1)}, u32[]{:S(2)}) copy-start(bf16[2,190]{1,0:T(2,128)(2,1)} %desc_ref.1) | copy-start | bytes 2284
  50.4 1.5 %copy-start = (bf16[960,960]{1,0:T(8,128)(2,1)S(1)}, bf16[960,960]{1,0:T(8,128)(2,1)}, u32[]{:S(2)}) copy-start(bf16[960,960]{1,0:T(8,128)(2,1)} %inv_ref.1) | copy-start | bytes 5529604

commit v2 on v0

v2 whole, which is shorter than its diff:
```python
import functools
import math

import jax
import jax.numpy as jnp
from jax import lax
from jax.experimental import pallas as pl
from jax.experimental.pallas import tpu as pltpu
from jax.sharding import PartitionSpec as P

MESH = pl.DeviceIdType.MESH
F32 = jnp.float32
BF16 = jnp.bfloat16
NC = 60
ND = 190
PB = 64
TR = 16
TL = 128
NZ = 16
NCH = 16
NP = 32
SLOTS = 32
PCOLS = 960

NT = (((1,), (1,)), ((), ()))
NN = (((1,), (0,)), ((), ()))


def dot(a, b, dims):
    return lax.dot_general(a, b, dims, preferred_element_type=F32)


def iota(shape, dim):
    return lax.broadcasted_iota(jnp.int32, shape, dim)


def onehot(cond):
    return jnp.where(cond, 1.0, 0.0).astype(BF16)


def own_blocks(jac, desc_ref, blk, stage, send1, own_ref):
    lane = iota((1, TL), 1)
    low = lane < 64
    sums = jnp.logical_and(lane % 64 >= 62, lane >= 0)
    blk[...] = jnp.zeros_like(blk)
    stage[...] = jnp.zeros_like(stage)
    jac32 = jac[...].astype(F32)
    for i in range(2):
        one = jac32[:, i, :]
        desc32 = desc_ref[i : i + 1, :].astype(F32)
        col = jnp.sum(one * desc32, axis=1, keepdims=True)
        high = col.astype(BF16).astype(F32)
        blk[i, 0, 0:NC, :] = one[:, 0:TL]
        blk[i, 0, NC : NC + 1, :] = desc32[:, 0:TL]
        blk[i, 1, 0:NC, 0 : ND - TL] = one[:, TL:ND]
        blk[i, 1, 0:NC, ND - TL : ND - TL + 1] = high
        blk[i, 1, 0:NC, ND - TL + 1 : ND - TL + 2] = col - high
        blk[i, 1, NC : NC + 1, 0 : ND - TL] = desc32[:, TL:ND]
        rest = blk[i, 1]
        both = rest + pltpu.roll(rest, 64, 1)
        is_desc = iota((PB, TL), 0) == NC
        rows = slice(PB * i, PB * i + PB)
        own_ref[rows, 0:TL] = blk[i, 0].astype(BF16)
        own_ref[rows, TL : 2 * TL] = jnp.where(sums, jnp.where(is_desc, -1.0, 0.0), both).astype(BF16)
        own_ref[rows, 2 * TL : 3 * TL] = rest.astype(BF16)
        even = blk[i, 1, pl.ds(0, NP, stride=2), :]
        odd = blk[i, 1, pl.ds(1, NP, stride=2), :]
        pair = jnp.where(low, even, pltpu.roll(odd, 64, 1))
        for q in range(NP):
            stage[q, 2 * i : 2 * i + 2, :] = blk[i, 0, 2 * q : 2 * q + 2, :]
            stage[q, 4 + i : 5 + i, :] = pair[q : q + 1, :]
    for q in range(NP):
        send1[q] = stage[q].astype(BF16)


def choices(order, panel, z, cap, step, total, one1, one2, over_ref, fast):
    base = panel[0] * TR
    lane = iota((8, TL), 1)
    sub = iota((8, TL), 0)
    parts = []
    line = jnp.zeros((8, TL), jnp.int32)
    for g in range(SLOTS // 8):
        part = jnp.zeros((8, TL), jnp.int32)
        for s in range(8 * g, 8 * g + 8):
            conf = order[base + s]
            part = jnp.where(sub == s - 8 * g, conf, part)
            line = jnp.where(lane == s, conf, line)
        parts.append(part)
    conf_col = jnp.concatenate(parts, axis=0)
    conf_row = jnp.concatenate([line] * 4, axis=0)
    plane_col = conf_col // (2 * NP)
    plane_row = conf_row // (2 * NP)
    slot_col = iota((SLOTS, TL), 0)
    slot_row = iota((SLOTS, TL), 1)
    same = plane_col == plane_row
    before = jnp.logical_and(same, slot_row < slot_col)
    rank_col = jnp.sum(jnp.where(before, 1.0, 0.0), axis=1, keepdims=True)
    if over_ref is not None:
        over_ref[0] = jnp.where(jnp.max(rank_col) >= cap, 1, 0)
    rank_col = jnp.broadcast_to(rank_col, (SLOTS, TL)).astype(jnp.int32)
    place = rank_col if fast else slot_col
    here = plane_col == z
    device = (conf_col // 2) % NP
    which = conf_col % 2
    finds = []
    for kind in range(3):
        at = device * TR + (2 * which + kind if kind < 2 else 4 + which)
        find = []
        for t in range(NP * TR // TL):
            find.append(jnp.logical_and(at == slot_row + TL * t, here))
        finds.append(onehot(jnp.concatenate(find, axis=1)))
        goal = plane_col * total + kind * step + place
        take = [goal == slot_row + TL * t for t in range(NZ * total // TL)]
        one2[kind * SLOTS : kind * SLOTS + SLOTS, :] = onehot(jnp.concatenate(take, axis=1))
    finds = jnp.concatenate(finds, axis=0)
    if fast:
        after = jnp.logical_and(same, slot_col < slot_row)
        rank_row = jnp.sum(jnp.where(after, 1.0, 0.0), axis=0, keepdims=True).astype(jnp.int32)
        row = iota((total, SLOTS), 0)
        packs = []
        for kind in range(3):
            here_row = plane_row[0:1, 0:SLOTS] == z
            hit = jnp.logical_and(row == kind * step + rank_row[:, 0:SLOTS], rank_row[:, 0:SLOTS] < cap)
            packs.append(jnp.where(jnp.logical_and(hit, here_row), 1.0, 0.0))
        pack = jnp.concatenate(packs, axis=1).astype(BF16)
        one1[...] = dot(pack, finds, NN).astype(BF16)
    else:
        one1[...] = finds


def exchange(cap, step, total, fast, *refs):
    order_ref, panel_ref, jac_ref, desc_ref, inv_ref = refs[:5]
    if fast:
        own_ref, all_ref, inv_out, perm_out, over_ref = refs[5:10]
        rest = refs[10:]
    else:
        own_ref, all_ref = refs[5:7]
        inv_out = perm_out = over_ref = None
        rest = refs[7:]
    (order, panel, jac, desc, inv, blk, stage, send1, got1, one1, send2, got2, one2, mine, ins,
     s1, r1, s2, r2, s4, r4, s5, r5) = rest
    z = lax.axis_index("row")
    col = lax.axis_index("col")
    core = col % 2
    chip = col // 2
    sib = chip * 2 + 1 - core

    barrier = pltpu.get_barrier_semaphore()
    far = sorted(range(1, NZ), key=lambda d: -min(d, NZ - d))
    for d in far:
        pl.semaphore_signal(barrier, inc=1, device_id=((z + d) % NZ, col), device_id_type=MESH)
    for d in range(1, NP):
        pl.semaphore_signal(barrier, inc=1, device_id=(z, (col + d) % NP), device_id_type=MESH)
    loads = [(jac_ref, jac), (desc_ref, desc), (order_ref, order), (panel_ref, panel)]
    if fast:
        loads.append((inv_ref, inv))
    loads = [pltpu.make_async_copy(a, b, ins.at[n]) for n, (a, b) in enumerate(loads)]
    for load in loads:
        load.start()
    loads[0].wait()
    loads[1].wait()
    own_blocks(jac, desc, blk, stage, send1, own_ref)
    pl.semaphore_wait(barrier, NZ - 1 + NP - 1)

    for d in range(1, NP):
        to = (col + d) % NP
        pltpu.make_async_remote_copy(
            send1.at[to], got1.at[col], s1, r1, device_id=(z, to), device_id_type=MESH
        ).start()
    got1[col] = send1[col]
    loads[2].wait()
    loads[3].wait()
    choices(order, panel, z, cap, step, total, one1, one2, over_ref, fast)
    if fast:
        at = iota((PCOLS, PCOLS), 1)
        perm_out[...] = onehot(iota((PCOLS, PCOLS), 0) == (at % TR) * NC + at // TR)
        loads[4].wait()
    pltpu.make_async_copy(got1.at[0 : NP - 1], got1.at[0 : NP - 1], r1).wait()

    send2[...] = dot(one1[...], got1[...].reshape(NP * TR, TL), NN).astype(BF16)
    for d in far:
        pltpu.make_async_remote_copy(
            send2, got2.at[z], s2, r2, device_id=((z + d) % NZ, col), device_id_type=MESH
        ).start()
    got2[z] = send2[...]
    if fast:

        @pl.loop(0, 3)
        def _(g):
            rows = pl.ds(pl.multiple_of(g * 320, 320), 320)
            inv_out[rows, :] = dot(inv[rows, :], perm_out[...], NN).astype(BF16)

    pltpu.make_async_copy(got2.at[0 : NZ - 1], got2.at[0 : NZ - 1], r2).wait()
    mine[...] = dot(one2[...], got2[...].reshape(NZ * total, TL), NN).astype(BF16)

    x, y = chip // 4, chip % 4
    steps = [(dx, dy) for dx in range(4) for dy in range(4) if dx or dy]
    steps.sort(key=lambda d: min(d[0], 4 - d[0]) + min(d[1], 4 - d[1]), reverse=True)
    for n, (dx, dy) in enumerate(steps):
        to = (((x + dx) % 4) * 4 + (y + dy) % 4) * 2 + core
        pltpu.make_async_remote_copy(
            mine, all_ref.at[core, chip], s4, r4.at[n], device_id=(z, to), device_id_type=MESH
        ).start()
    pltpu.make_async_remote_copy(
        mine, all_ref.at[core, chip], s5, r5, device_id=(z, sib), device_id_type=MESH
    ).start()
    all_ref[core, chip] = mine[...]
    for n, (dx, dy) in reversed(list(enumerate(steps))):
        source = ((x + 4 - dx) % 4) * 4 + (y + 4 - dy) % 4
        landed = all_ref.at[core, source]
        pltpu.make_async_copy(landed, landed, r4.at[n]).wait()
        pltpu.make_async_remote_copy(
            landed, landed, s5, r5, device_id=(z, sib), device_id_type=MESH
        ).start()
    other = all_ref.at[1 - core]
    pltpu.make_async_copy(other, other, r5).wait()

    pltpu.make_async_copy(got1.at[0 : NP - 1], got1.at[0 : NP - 1], s1).wait()
    pltpu.make_async_copy(got2.at[0 : NZ - 1], got2.at[0 : NZ - 1], s2).wait()
    pltpu.make_async_copy(all_ref.at[0, 0:15], all_ref.at[0, 0:15], s4).wait()
    pltpu.make_async_copy(other, other, s5).wait()


def compute(own_ref, all_ref, inv_ref, perm_ref, factor_ref, next_ref, rhs, lhs, lhs2, dexp, cross, solved, outs):
    width = 2.0 * math.sqrt(2.0 * ND)
    lane = iota((TR, TL), 1)
    low = lane < 64
    sums = lane % 64 >= 62
    last = jnp.logical_and(lane >= 62, low)

    def piece(row, kind, half):
        p = row // 2
        first = (kind * 2 + half) * TR
        return all_ref[p % 2, p // 2, first : first + TR, :]

    ds = []
    for half in range(2):
        for p in range(NC // 2 + 1):
            rest = piece(2 * p, 2, half).astype(F32)
            turned = pltpu.roll(rest, 64, 1)
            for odd in range(2):
                row = 2 * p + odd
                if row > NC:
                    continue
                xt = piece(row, odd, half)
                rows = slice(TR * row, TR * row + TR)
                mine = turned if odd else rest
                if row < NC:
                    rhs[half, rows, 0:TL] = xt
                    rhs[half, rows, TL : 2 * TL] = jnp.where(low != (odd == 1), rest, 0.0).astype(BF16)
                if half == 0:
                    both = jnp.where(low != (odd == 1), rest, turned)
                    lhs[rows, 0:TL] = xt
                    lhs[rows, TL : 2 * TL] = jnp.where(sums, -1.0 if row == NC else 0.0, both).astype(BF16)
                    if row < NC:
                        lhs2[rows, 0:TL] = xt
                        lhs2[rows, TL : 2 * TL] = mine.astype(BF16)
                if row == NC:
                    d0, d1 = xt.astype(F32), jnp.where(low, rest, 0.0)
                    ds.append((d0, d1))
                    e1 = jnp.where(last, -1.0, d1).astype(BF16)
                    for t in range(TL // TR):
                        to = slice(TL * half + TR * t, TL * half + TR * t + TR)
                        dexp[to, 0:TL] = xt
                        dexp[to, TL : 2 * TL] = e1

    zero = jnp.zeros((6, TL), F32)
    own_d = [own_ref[PB * i + NC - 12 : PB * i + PB - 0, :].astype(F32)[12:13] for i in range(2)]
    d0s = jnp.concatenate([ds[0][0]] + [d[:, 0:TL] for d in own_d] + [zero], axis=0)
    d1s = jnp.concatenate([ds[0][1]] + [jnp.where(low[0:1], d[:, 2 * TL :], 0.0) for d in own_d] + [zero], axis=0)
    f1s, f2s = [], []
    lane24 = iota((24, TL), 1) % TR
    for half in range(2):
        dist = jnp.zeros((24, TL), F32)
        for b in range(TR):
            u0 = d0s - ds[half][0][b : b + 1, :]
            u1 = d1s - ds[half][1][b : b + 1, :]
            dist = jnp.where(lane24 == b, jnp.sum(u0 * u0 + u1 * u1, axis=1, keepdims=True), dist)
        scaled = (math.sqrt(5.0) / width) * jnp.sqrt(dist)
        decay = jnp.exp(-scaled)
        f1s.append(decay * (1.0 + scaled))
        f2s.append(decay * (5.0 / (width * width)))

    def wide(tile):
        return jnp.concatenate([tile] * 8, axis=1)[:, 0:PCOLS]

    own_lhs = own_ref[:, 0 : 2 * TL]
    own_lhs2 = jnp.concatenate([own_ref[:, 0:TL], own_ref[:, 2 * TL :]], axis=1)
    prod2 = dot(own_lhs2, dexp[...], NT)
    tiles = []
    for half in range(2):
        prod = dot(own_lhs, rhs[half], NT)
        parts = []
        for i in range(2):
            rows = slice(PB * i, PB * i + PB)
            f1 = wide(f1s[half][TR + i : TR + i + 1, :])
            qq = wide(f2s[half][TR + i : TR + i + 1, :]) * prod[PB * i + NC : PB * i + NC + 1, :]
            p = wide(prod2[rows, TL * half : TL * half + TL])
            parts.append(prod[rows, :] * f1 + p * qq)
        tiles.append(jnp.concatenate(parts, axis=0))
    factor = dot(tiles[0].astype(BF16), inv_ref[...], NT)
    outs[0:NC, :] = factor[0:NC, :]
    outs[NC : 2 * NC, :] = factor[PB : PB + NC, :]
    factor_ref[...] = outs[...].astype(BF16)

    qq = wide(f2s[1][0:TR, :]) * dot(lhs[PCOLS : PCOLS + TR, :], rhs[1], NT)
    f1 = wide(f1s[1][0:TR, :])

    @pl.loop(0, 4)
    def _(g):
        rows = pl.ds(pl.multiple_of(g * 240, 240), 240)
        a = dot(lhs[rows, :], rhs[1], NT)
        b = dot(lhs2[rows, :], dexp[TL : 2 * TL, :], NT)
        got = []
        for n in range(15):
            part = slice(TR * n, TR * n + TR)
            got.append((a[part, :] * f1 + wide(b[part, :]) * qq).astype(BF16))
        cross[rows, :] = jnp.concatenate(got, axis=0)

    @pl.loop(0, 3)
    def _(g):
        rows = pl.ds(pl.multiple_of(g * 320, 320), 320)
        solved[rows, :] = dot(inv_ref[rows, :], cross[...], NN).astype(BF16)

    updated = (tiles[1] - dot(factor.astype(BF16), solved[...], NN)).astype(BF16)
    final = dot(updated, perm_ref[...], NT)
    outs[0:NC, :] = final[0:NC, :]
    outs[NC : 2 * NC, :] = final[PB : PB + NC, :]
    next_ref[...] = outs[...].astype(BF16)


VM = pl.BlockSpec(memory_space=pltpu.VMEM)
ANY = pl.BlockSpec(memory_space=pl.ANY)


def run_exchange(fast, order, panel, jac, desc, inv):
    cap, step, total = (10, 10, 32) if fast else (32, 32, 96)
    square = jax.ShapeDtypeStruct((PCOLS, PCOLS), BF16)
    outs = (
        jax.ShapeDtypeStruct((2 * PB, 3 * TL), BF16),
        jax.ShapeDtypeStruct((2, NCH, 3 * SLOTS, TL), BF16),
    )
    specs = (VM, VM)
    if fast:
        outs += (square, square, jax.ShapeDtypeStruct((1,), jnp.int32))
        specs += (VM, VM, pl.BlockSpec(memory_space=pltpu.SMEM))
    dma = pltpu.SemaphoreType.DMA
    return pl.pallas_call(
        functools.partial(exchange, cap, step, total, fast),
        name="exchange" if fast else "exchange_full",
        out_shape=outs,
        in_specs=[ANY] * 5,
        out_specs=specs,
        scratch_shapes=[
            pltpu.SMEM((NZ * 2 * NP,), jnp.int32),
            pltpu.SMEM((1,), jnp.int32),
            pltpu.VMEM(jac.shape, BF16),
            pltpu.VMEM(desc.shape, BF16),
            pltpu.VMEM((PCOLS, PCOLS) if fast else (TR, TL), BF16),
            pltpu.VMEM((2, 2, PB, TL), F32),
            pltpu.VMEM((NP, TR, TL), F32),
            pltpu.VMEM((NP, TR, TL), BF16),
            pltpu.VMEM((NP, TR, TL), BF16),
            pltpu.VMEM((total, NP * TR), BF16),
            pltpu.VMEM((total, TL), BF16),
            pltpu.VMEM((NZ, total, TL), BF16),
            pltpu.VMEM((3 * SLOTS, NZ * total), BF16),
            pltpu.VMEM((3 * SLOTS, TL), BF16),
            dma((5,)), dma, dma, dma, dma, dma, dma((NCH - 1,)), dma, dma,
        ],
        compiler_params=pltpu.CompilerParams(
            collective_id=0 if fast else 1, has_side_effects=True, vmem_limit_bytes=24 * 2**20
        ),
    )(order, panel, jac, desc, inv)


def run_compute(own, everything, inv, perm):
    rows = 2 * NC
    return pl.pallas_call(
        compute,
        name="compute",
        out_shape=(jax.ShapeDtypeStruct((rows, PCOLS), BF16),) * 2,
        in_specs=[VM] * 4,
        out_specs=(VM, VM),
        scratch_shapes=[
            pltpu.VMEM((2, PCOLS, 2 * TL), BF16),
            pltpu.VMEM((PCOLS + TR, 2 * TL), BF16),
            pltpu.VMEM((PCOLS, 2 * TL), BF16),
            pltpu.VMEM((2 * TL, 2 * TL), BF16),
            pltpu.VMEM((PCOLS, PCOLS), BF16),
            pltpu.VMEM((PCOLS, PCOLS), BF16),
            pltpu.VMEM((rows, PCOLS), F32),
        ],
        compiler_params=pltpu.CompilerParams(vmem_limit_bytes=40 * 2**20),
    )(own, everything, inv, perm)


def shards(jacobians, descriptors, block_inverse, tile_order, panel):
    jac = jnp.transpose(jacobians, (1, 0, 2))
    args = (tile_order, panel, jac, descriptors, block_inverse)
    own, few, inv, perm, over = run_exchange(True, *args)

    def usual():
        return run_compute(own, few, inv, perm)

    def crowded():
        again, everything = run_exchange(False, *args)
        return run_compute(again, everything, inv, perm)

    return lax.cond(over[0] == 0, usual, crowded)


def solution(mesh):
    placed = (P(("row", "col"), None, None), P(("row", "col"), None), P(), P(), P())
    return jax.shard_map(
        shards,
        mesh=mesh,
        in_specs=placed,
        out_specs=(P(("row", "col"), None), P(("row", "col"), None)),
        check_vma=False,
    )
```

time: 223 us -> 48.4 us (0.22)
  the two profiles are of different devices: /device:TPU:4 before, /device:TPU:1 now
where the time goes in v2:
time: 48.4 us; the launch traced here: 48.3 us
  Pallas kernels  46.1 us (95%)
  between operations  2.17 us (4%)
    pallas_call x1, Pallas kernels, run_exchange(): pl.pallas_call(functools.partial(exchange, cap, step, total, fast), name=...  38.9 us
    pallas_call x1, Pallas kernels, run_compute(): pl.pallas_call(compute, name='compute', out_shape=(jax.ShapeDtypeStruct((...  7.19 us

profile of v2, /device:TPU:1, one launch (start us, length us, event | category | flops | bytes accessed | tf_op | source)
XLA Modules:
  0.0 48.3 jit_solution(9977356857665981853)
XLA Ops:
  0.6 0.0 copy-start.2
  0.6 0.0 copy-start
  0.7 0.0 copy-start.3
  0.7 0.0 copy-start.1
  1.5 38.9 %exchange.1 = (bf16[128,384]{1,0:T(8,128)(2,1)S(1)}, bf16[2,16,96,128]{3,2,1,0:T(8,128)(2,1)S(1)}, bf16[960,960]{1,0:T(8,128)(2,1)S(1)}, bf16[960,960]{1,0:T(8,128)(2,1)S(1)}, s32[1]{0:T(128)}) custom-call(s32[1024]{0:T(1024)} %refs_0_.1, s32[1]{0:T(128)S(6)} %copy.15.refs_1_, bf16[60,2,190]{2,1,0:T(2,128)(2,1)} %bitcast.2, bf16[2,190]{1,0:T(2,128)(2,1)} %refs_3_.1, ...), custom_call_target="tpu_custom_call" | custom-call | tf_op jit(solution)/shard_map/exchange/pallas_call | solution.py:348
  41.0 0.0 copy-done.2
  41.1 0.0 copy-done
  41.1 0.0 copy-done.3
  41.1 0.0 copy-done.1
  41.1 7.2 %conditional.1 = ((bf16[120,960]{1,0:T(8,128)(2,1)}, bf16[120,960]{1,0:T(8,128)(2,1)})) conditional(s32[]{:T(128)} %bitcast.1, (s32[1024]{0:T(1024)S(1)}, s32[1]{0:T(128)}, bf16[60,2,190]{2,1,0:T(2,128)(2,1)S(1)}, bf16[2,190]{1,0:T(2,128)(2,1)S(1)}, bf16[960,960]{1,0:T(8,128)(2,1)S(1)}, /*index=5*/bf16[960,960]{1,0:T(8,128)(2,1)S(1)}, ...), branch_computations={%region_0.0_spmd, %region_1.0_spmd} | conditional | bytes 8 | solution.py:410
  41.1 7.2 %compute.3 = (bf16[120,960]{1,0:T(8,128)(2,1)}, bf16[120,960]{1,0:T(8,128)(2,1)}) custom-call(bf16[128,384]{1,0:T(8,128)(2,1)S(1)} %get-tuple-element.31.own_ref, bf16[2,16,96,128]{3,2,1,0:T(8,128)(2,1)S(1)} %get-tuple-element.32.all_ref, bf16[960,960]{1,0:T(8,128)(2,1)S(1)} %get-tuple-element.33.inv_ref, bf16[960,960]{1,0:T(8,128)(2,1)S(1)} %get-tuple-element.34.perm_ref), custom_call_target="tpu_custom_call" | custom-call | tf_op jit(solution)/shard_map/cond/branch_1_fun/compute/pallas_call | solution.py:379
Async XLA Ops:
  0.6 40.4 %copy-start.2 = (s32[1024]{0:T(1024)S(1)}, s32[1024]{0:T(1024)}, u32[]{:S(2)}) copy-start(s32[1024]{0:T(1024)} %refs_0_.1) | copy-start | bytes 12292
  0.6 40.4 %copy-start = (bf16[960,960]{1,0:T(8,128)(2,1)S(1)}, bf16[960,960]{1,0:T(8,128)(2,1)}, u32[]{:S(2)}) copy-start(bf16[960,960]{1,0:T(8,128)(2,1)} %refs_4_.1) | copy-start | bytes 5529604
  0.7 40.4 %copy-start.3 = (bf16[2,190]{1,0:T(2,128)(2,1)S(1)}, bf16[2,190]{1,0:T(2,128)(2,1)}, u32[]{:S(2)}) copy-start(bf16[2,190]{1,0:T(2,128)(2,1)} %refs_3_.1) | copy-start | bytes 2284
  0.7 40.4 %copy-start.1 = (bf16[2,60,190]{2,0,1:T(2,128)(2,1)S(1)}, bf16[2,60,190]{2,0,1:T(2,128)(2,1)}, u32[]{:S(2)}) copy-start(bf16[2,60,190]{2,0,1:T(2,128)(2,1)} %param.7) | copy-start | bytes 136804

commit v3 on v2

--- a/solution.py
+++ b/solution.py
@@ -221,7 +221,7 @@
     pltpu.make_async_copy(other, other, s5).wait()
 
 
-def compute(own_ref, all_ref, inv_ref, perm_ref, factor_ref, next_ref, rhs, lhs, lhs2, dexp, cross, solved, outs):
+def compute(own_ref, all_ref, inv_ref, perm_ref, factor_ref, next_ref, rhs, lhs, lhs2, dexp, cross, outs):
     width = 2.0 * math.sqrt(2.0 * ND)
     lane = iota((TR, TL), 1)
     low = lane < 64
@@ -302,13 +302,20 @@
     outs[0:NC, :] = factor[0:NC, :]
     outs[NC : 2 * NC, :] = factor[PB : PB + NC, :]
     factor_ref[...] = outs[...].astype(BF16)
+    most = jnp.max(jnp.abs(factor), axis=1, keepdims=True)
+    scale = jnp.ones_like(most)
+    back = jnp.ones_like(most)
+    for _ in range(4):
+        large = most * scale > 2.0**24
+        scale = jnp.where(large, scale * 2.0**-24, scale)
+        back = jnp.where(large, back * 2.0**24, back)
+    scaled_factor = (factor.astype(BF16).astype(F32) * scale).astype(BF16)
 
     qq = wide(f2s[1][0:TR, :]) * dot(lhs[PCOLS : PCOLS + TR, :], rhs[1], NT)
     f1 = wide(f1s[1][0:TR, :])
 
-    @pl.loop(0, 4)
-    def _(g):
-        rows = pl.ds(pl.multiple_of(g * 240, 240), 240)
+    for g in range(4):
+        rows = slice(240 * g, 240 * g + 240)
         a = dot(lhs[rows, :], rhs[1], NT)
         b = dot(lhs2[rows, :], dexp[TL : 2 * TL, :], NT)
         got = []
@@ -317,12 +324,12 @@
             got.append((a[part, :] * f1 + wide(b[part, :]) * qq).astype(BF16))
         cross[rows, :] = jnp.concatenate(got, axis=0)
 
-    @pl.loop(0, 3)
-    def _(g):
-        rows = pl.ds(pl.multiple_of(g * 320, 320), 320)
-        solved[rows, :] = dot(inv_ref[rows, :], cross[...], NN).astype(BF16)
-
-    updated = (tiles[1] - dot(factor.astype(BF16), solved[...], NN)).astype(BF16)
+    middle = dot(scaled_factor, inv_ref[...], NN)
+    high = middle.astype(BF16)
+    both = jnp.concatenate([high, (middle - high.astype(F32)).astype(BF16)], axis=0)
+    change = dot(both, cross[...], NN)
+    change = (change[0:TL, :] + change[TL : 2 * TL, :]) * back
+    updated = (tiles[1] - change).astype(BF16)
     final = dot(updated, perm_ref[...], NT)
     outs[0:NC, :] = final[0:NC, :]
     outs[NC : 2 * NC, :] = final[PB : PB + NC, :]
@@ -330,7 +337,7 @@
 
 
 VM = pl.BlockSpec(memory_space=pltpu.VMEM)
-ANY = pl.BlockSpec(memory_space=pl.ANY)
+HBM = pl.BlockSpec(memory_space=pltpu.HBM)
 
 
 def run_exchange(fast, order, panel, jac, desc, inv):
@@ -349,7 +356,7 @@
         functools.partial(exchange, cap, step, total, fast),
         name="exchange" if fast else "exchange_full",
         out_shape=outs,
-        in_specs=[ANY] * 5,
+        in_specs=[HBM] * 5,
         out_specs=specs,
         scratch_shapes=[
             pltpu.SMEM((NZ * 2 * NP,), jnp.int32),
@@ -388,7 +395,6 @@
             pltpu.VMEM((PCOLS, 2 * TL), BF16),
             pltpu.VMEM((2 * TL, 2 * TL), BF16),
             pltpu.VMEM((PCOLS, PCOLS), BF16),
-            pltpu.VMEM((PCOLS, PCOLS), BF16),
             pltpu.VMEM((rows, PCOLS), F32),
         ],
         compiler_params=pltpu.CompilerParams(vmem_limit_bytes=40 * 2**20),
@@ -400,14 +406,16 @@
     args = (tile_order, panel, jac, descriptors, block_inverse)
     own, few, inv, perm, over = run_exchange(True, *args)
 
-    def usual():
-        return run_compute(own, few, inv, perm)
-
-    def crowded():
+    outs = run_compute(own, few, inv, perm)
+
+    def usual(outs):
+        return outs
+
+    def crowded(outs):
         again, everything = run_exchange(False, *args)
         return run_compute(again, everything, inv, perm)
 
-    return lax.cond(over[0] == 0, usual, crowded)
+    return lax.cond(over[0] == 0, usual, crowded, outs)
 
 
 def solution(mesh):

time: 48.4 us -> 45.4 us (0.938)
  Pallas kernels: 46.1 us -> 43.3 us
    pallas_call x1, Pallas kernels: 7.19 us -> 4.36 us  [run_compute(): pl.pallas_call(compute, name='compute', out_shape=(jax.ShapeDtypeStruct((...]
where the time goes in v3:
time: 45.4 us; the launch traced here: 45.2 us
  Pallas kernels  43.3 us (95%)
  between operations  1.89 us (4%)
    pallas_call x1, Pallas kernels, run_exchange(): pl.pallas_call(functools.partial(exchange, cap, step, total, fast), name=...  38.9 us
    pallas_call x1, Pallas kernels, run_compute(): pl.pallas_call(compute, name='compute', out_shape=(jax.ShapeDtypeStruct((...  4.36 us

profile of v3, /device:TPU:1, one launch (start us, length us, event | category | flops | bytes accessed | tf_op | source)
XLA Modules:
  0.0 45.2 jit_solution(12634232324942352861)
XLA Ops:
  1.3 38.9 %exchange.1 = (bf16[128,384]{1,0:T(8,128)(2,1)S(1)}, bf16[2,16,96,128]{3,2,1,0:T(8,128)(2,1)S(1)}, bf16[960,960]{1,0:T(8,128)(2,1)S(1)}, bf16[960,960]{1,0:T(8,128)(2,1)S(1)}, s32[1]{0:T(128)}) custom-call(s32[1024]{0:T(1024)} %refs_0_.1, s32[1]{0:T(128)S(6)} %copy.15.refs_1_, bf16[60,2,190]{2,1,0:T(2,128)(2,1)} %bitcast.2, bf16[2,190]{1,0:T(2,128)(2,1)} %refs_3_.1, ...), custom_call_target="tpu_custom_call" | custom-call | tf_op jit(solution)/shard_map/exchange/pallas_call | solution.py:355
  40.8 0.0 copy-start
  40.8 0.0 copy-start.1
  40.8 0.0 copy-start.2
  40.8 0.0 copy-start.3
  40.8 4.4 %compute.3 = (bf16[120,960]{1,0:T(8,128)(2,1)}, bf16[120,960]{1,0:T(8,128)(2,1)}) custom-call(bf16[128,384]{1,0:T(8,128)(2,1)S(1)} %get-tuple-element.37.own_ref, bf16[2,16,96,128]{3,2,1,0:T(8,128)(2,1)S(1)} %get-tuple-element.38.all_ref, bf16[960,960]{1,0:T(8,128)(2,1)S(1)} %get-tuple-element.35.inv_ref, bf16[960,960]{1,0:T(8,128)(2,1)S(1)} %get-tuple-element.36.perm_ref), custom_call_target="tpu_custom_call" | custom-call | tf_op jit(solution)/shard_map/compute/pallas_call | solution.py:386
  45.2 0.0 copy-done
  45.2 0.0 copy-done.1
  45.2 0.0 copy-done.2
  45.2 0.0 copy-done.3
  (1 shorter events, 0.0 us)
Async XLA Ops:
  40.8 4.4 %copy-start = (bf16[960,960]{1,0:T(8,128)(2,1)S(1)}, bf16[960,960]{1,0:T(8,128)(2,1)}, u32[]{:S(2)}) copy-start(bf16[960,960]{1,0:T(8,128)(2,1)} %refs_4_.1) | copy-start | bytes 5529604
  40.8 4.4 %copy-start.1 = (bf16[2,60,190]{2,0,1:T(2,128)(2,1)S(1)}, bf16[2,60,190]{2,0,1:T(2,128)(2,1)}, u32[]{:S(2)}) copy-start(bf16[2,60,190]{2,0,1:T(2,128)(2,1)} %param.7) | copy-start | bytes 136804
  40.8 4.4 %copy-start.2 = (s32[1024]{0:T(1024)S(1)}, s32[1024]{0:T(1024)}, u32[]{:S(2)}) copy-start(s32[1024]{0:T(1024)} %refs_0_.1) | copy-start | bytes 12292
  40.8 4.4 %copy-start.3 = (bf16[2,190]{1,0:T(2,128)(2,1)S(1)}, bf16[2,190]{1,0:T(2,128)(2,1)}, u32[]{:S(2)}) copy-start(bf16[2,190]{1,0:T(2,128)(2,1)} %refs_3_.1) | copy-start | bytes 2284

commit v4 on v3

--- a/solution.py
+++ b/solution.py
@@ -16,6 +16,7 @@
 PB = 64
 TR = 16
 TL = 128
+PR = 8
 NZ = 16
 NCH = 16
 NP = 32
@@ -104,9 +105,9 @@
     which = conf_col % 2
     finds = []
     for kind in range(3):
-        at = device * TR + (2 * which + kind if kind < 2 else 4 + which)
+        at = device * PR + (2 * which + kind if kind < 2 else 4 + which)
         find = []
-        for t in range(NP * TR // TL):
+        for t in range(NP * PR // TL):
             find.append(jnp.logical_and(at == slot_row + TL * t, here))
         finds.append(onehot(jnp.concatenate(find, axis=1)))
         goal = plane_col * total + kind * step + place
@@ -116,7 +117,7 @@
     if fast:
         after = jnp.logical_and(same, slot_col < slot_row)
         rank_row = jnp.sum(jnp.where(after, 1.0, 0.0), axis=0, keepdims=True).astype(jnp.int32)
-        row = iota((total, SLOTS), 0)
+        row = iota((one1.shape[0], SLOTS), 0)
         packs = []
         for kind in range(3):
             here_row = plane_row[0:1, 0:SLOTS] == z
@@ -162,8 +163,13 @@
     own_blocks(jac, desc, blk, stage, send1, own_ref)
     pl.semaphore_wait(barrier, NZ - 1 + NP - 1)
 
-    for d in range(1, NP):
-        to = (col + d) % NP
+    x, y = chip // 4, chip % 4
+    steps = [(dx, dy) for dx in range(4) for dy in range(4)]
+    steps.sort(key=lambda d: min(d[0], 4 - d[0]) + min(d[1], 4 - d[1]), reverse=True)
+    for dx, dy, dc in [(dx, dy, dc) for dx, dy in steps for dc in range(2)]:
+        if not (dx or dy or dc):
+            continue
+        to = (((x + dx) % 4) * 4 + (y + dy) % 4) * 2 + (core + dc) % 2
         pltpu.make_async_remote_copy(
             send1.at[to], got1.at[col], s1, r1, device_id=(z, to), device_id_type=MESH
         ).start()
@@ -177,7 +183,8 @@
         loads[4].wait()
     pltpu.make_async_copy(got1.at[0 : NP - 1], got1.at[0 : NP - 1], r1).wait()
 
-    send2[...] = dot(one1[...], got1[...].reshape(NP * TR, TL), NN).astype(BF16)
+    held = got1[...].astype(F32).reshape(NP * PR, TL).astype(BF16)
+    send2[...] = dot(one1[...], held, NN)[0:total, :].astype(BF16)
     for d in far:
         pltpu.make_async_remote_copy(
             send2, got2.at[z], s2, r2, device_id=((z + d) % NZ, col), device_id_type=MESH
@@ -191,11 +198,10 @@
             inv_out[rows, :] = dot(inv[rows, :], perm_out[...], NN).astype(BF16)
 
     pltpu.make_async_copy(got2.at[0 : NZ - 1], got2.at[0 : NZ - 1], r2).wait()
-    mine[...] = dot(one2[...], got2[...].reshape(NZ * total, TL), NN).astype(BF16)
-
-    x, y = chip // 4, chip % 4
-    steps = [(dx, dy) for dx in range(4) for dy in range(4) if dx or dy]
-    steps.sort(key=lambda d: min(d[0], 4 - d[0]) + min(d[1], 4 - d[1]), reverse=True)
+    held = got2[...].astype(F32).reshape(NZ * total, TL).astype(BF16)
+    mine[...] = dot(one2[...], held, NN).astype(BF16)
+
+    steps = steps[:-1]
     for n, (dx, dy) in enumerate(steps):
         to = (((x + dx) % 4) * 4 + (y + dy) % 4) * 2 + core
         pltpu.make_async_remote_copy(
@@ -341,7 +347,7 @@
 
 
 def run_exchange(fast, order, panel, jac, desc, inv):
-    cap, step, total = (10, 10, 32) if fast else (32, 32, 96)
+    cap, step, total = (8, 8, 24) if fast else (32, 32, 96)
     square = jax.ShapeDtypeStruct((PCOLS, PCOLS), BF16)
     outs = (
         jax.ShapeDtypeStruct((2 * PB, 3 * TL), BF16),
@@ -365,10 +371,10 @@
             pltpu.VMEM(desc.shape, BF16),
             pltpu.VMEM((PCOLS, PCOLS) if fast else (TR, TL), BF16),
             pltpu.VMEM((2, 2, PB, TL), F32),
-            pltpu.VMEM((NP, TR, TL), F32),
-            pltpu.VMEM((NP, TR, TL), BF16),
-            pltpu.VMEM((NP, TR, TL), BF16),
-            pltpu.VMEM((total, NP * TR), BF16),
+            pltpu.VMEM((NP, PR, TL), F32),
+            pltpu.VMEM((NP, PR, TL), BF16),
+            pltpu.VMEM((NP, PR, TL), BF16),
+            pltpu.VMEM((-(-total // TR) * TR, NP * PR), BF16),
             pltpu.VMEM((total, TL), BF16),
             pltpu.VMEM((NZ, total, TL), BF16),
             pltpu.VMEM((3 * SLOTS, NZ * total), BF16),

time: 45.4 us -> 43.9 us (0.967)
  Pallas kernels: 43.3 us -> 41.8 us
    pallas_call x1, Pallas kernels: 38.9 us -> 37.4 us  [run_exchange(): pl.pallas_call(functools.partial(exchange, cap, step, total, fast), name=...]
where the time goes in v4:
time: 43.9 us; the launch traced here: 43.7 us
  Pallas kernels  41.8 us (95%)
  between operations  1.89 us (4%)
    pallas_call x1, Pallas kernels, run_exchange(): pl.pallas_call(functools.partial(exchange, cap, step, total, fast), name=...  37.4 us
    pallas_call x1, Pallas kernels, run_compute(): pl.pallas_call(compute, name='compute', out_shape=(jax.ShapeDtypeStruct((...  4.36 us

profile of v4, /device:TPU:1, one launch (start us, length us, event | category | flops | bytes accessed | tf_op | source)
XLA Modules:
  0.0 43.7 jit_solution(13962949584710298359)
XLA Ops:
  1.3 37.4 %exchange.1 = (bf16[128,384]{1,0:T(8,128)(2,1)S(1)}, bf16[2,16,96,128]{3,2,1,0:T(8,128)(2,1)S(1)}, bf16[960,960]{1,0:T(8,128)(2,1)S(1)}, bf16[960,960]{1,0:T(8,128)(2,1)S(1)}, s32[1]{0:T(128)}) custom-call(s32[1024]{0:T(1024)} %refs_0_.1, s32[1]{0:T(128)S(6)} %copy.15.refs_1_, bf16[60,2,190]{2,1,0:T(2,128)(2,1)} %bitcast.2, bf16[2,190]{1,0:T(2,128)(2,1)} %refs_3_.1, ...), custom_call_target="tpu_custom_call" | custom-call | tf_op jit(solution)/shard_map/exchange/pallas_call | solution.py:361
  39.3 0.0 copy-start
  39.3 0.0 copy-start.1
  39.3 0.0 copy-start.2
  39.3 0.0 copy-start.3
  39.3 4.4 %compute.3 = (bf16[120,960]{1,0:T(8,128)(2,1)}, bf16[120,960]{1,0:T(8,128)(2,1)}) custom-call(bf16[128,384]{1,0:T(8,128)(2,1)S(1)} %get-tuple-element.37.own_ref, bf16[2,16,96,128]{3,2,1,0:T(8,128)(2,1)S(1)} %get-tuple-element.38.all_ref, bf16[960,960]{1,0:T(8,128)(2,1)S(1)} %get-tuple-element.35.inv_ref, bf16[960,960]{1,0:T(8,128)(2,1)S(1)} %get-tuple-element.36.perm_ref), custom_call_target="tpu_custom_call" | custom-call | tf_op jit(solution)/shard_map/compute/pallas_call | solution.py:392
  43.7 0.0 copy-done
  43.7 0.0 copy-done.1
  43.7 0.0 copy-done.2
  43.7 0.0 copy-done.3
  (1 shorter events, 0.0 us)
Async XLA Ops:
  39.3 4.4 %copy-start = (bf16[960,960]{1,0:T(8,128)(2,1)S(1)}, bf16[960,960]{1,0:T(8,128)(2,1)}, u32[]{:S(2)}) copy-start(bf16[960,960]{1,0:T(8,128)(2,1)} %refs_4_.1) | copy-start | bytes 5529604
  39.3 4.4 %copy-start.1 = (bf16[2,60,190]{2,0,1:T(2,128)(2,1)S(1)}, bf16[2,60,190]{2,0,1:T(2,128)(2,1)}, u32[]{:S(2)}) copy-start(bf16[2,60,190]{2,0,1:T(2,128)(2,1)} %param.7) | copy-start | bytes 136804
  39.3 4.4 %copy-start.2 = (s32[1024]{0:T(1024)S(1)}, s32[1024]{0:T(1024)}, u32[]{:S(2)}) copy-start(s32[1024]{0:T(1024)} %refs_0_.1) | copy-start | bytes 12292
  39.3 4.4 %copy-start.3 = (bf16[2,190]{1,0:T(2,128)(2,1)S(1)}, bf16[2,190]{1,0:T(2,128)(2,1)}, u32[]{:S(2)}) copy-start(bf16[2,190]{1,0:T(2,128)(2,1)} %refs_3_.1) | copy-start | bytes 2284

commit v5 on v4

--- a/solution.py
+++ b/solution.py
@@ -139,7 +139,7 @@
         inv_out = perm_out = over_ref = None
         rest = refs[7:]
     (order, panel, jac, desc, inv, blk, stage, send1, got1, one1, send2, got2, one2, mine, ins,
-     s1, r1, s2, r2, s4, r4, s5, r5) = rest
+     s1, r1, s2, r2, s4, r4, s5, r5, plane, line) = rest
     z = lax.axis_index("row")
     col = lax.axis_index("col")
     core = col % 2
@@ -149,9 +149,14 @@
     barrier = pltpu.get_barrier_semaphore()
     far = sorted(range(1, NZ), key=lambda d: -min(d, NZ - d))
     for d in far:
-        pl.semaphore_signal(barrier, inc=1, device_id=((z + d) % NZ, col), device_id_type=MESH)
-    for d in range(1, NP):
-        pl.semaphore_signal(barrier, inc=1, device_id=(z, (col + d) % NP), device_id_type=MESH)
+        pl.semaphore_signal(barrier, inc=1, device_id=((z + d) % NZ, 2 * chip + 1), device_id_type=MESH)
+    for d in range(1, NCH):
+        pl.semaphore_signal(barrier, inc=1, device_id=(z, (chip + d) % NCH * 2), device_id_type=MESH)
+
+    @pl.when(core == 1)
+    def _():
+        pl.semaphore_signal(barrier, inc=1, device_id=(z, sib), device_id_type=MESH)
+
     loads = [(jac_ref, jac), (desc_ref, desc), (order_ref, order), (panel_ref, panel)]
     if fast:
         loads.append((inv_ref, inv))
@@ -161,7 +166,15 @@
     loads[0].wait()
     loads[1].wait()
     own_blocks(jac, desc, blk, stage, send1, own_ref)
-    pl.semaphore_wait(barrier, NZ - 1 + NP - 1)
+
+    @pl.when(core == 0)
+    def _():
+        pl.semaphore_wait(barrier, NP - 1)
+        pl.semaphore_signal(plane, inc=1, device_id=(z, sib), device_id_type=MESH)
+
+    @pl.when(core == 1)
+    def _():
+        pl.semaphore_wait(plane, 1)
 
     x, y = chip // 4, chip % 4
     steps = [(dx, dy) for dx in range(4) for dy in range(4)]
@@ -181,10 +194,20 @@
         at = iota((PCOLS, PCOLS), 1)
         perm_out[...] = onehot(iota((PCOLS, PCOLS), 0) == (at % TR) * NC + at // TR)
         loads[4].wait()
+
+    @pl.when(core == 1)
+    def _():
+        pl.semaphore_wait(barrier, 2 * (NZ - 1))
+        pl.semaphore_signal(line, inc=1, device_id=(z, sib), device_id_type=MESH)
+
+    @pl.when(core == 0)
+    def _():
+        pl.semaphore_wait(line, 1)
+
     pltpu.make_async_copy(got1.at[0 : NP - 1], got1.at[0 : NP - 1], r1).wait()
 
     held = got1[...].astype(F32).reshape(NP * PR, TL).astype(BF16)
-    send2[...] = dot(one1[...], held, NN)[0:total, :].astype(BF16)
+    send2[...] = dot(one1[...], held, NN)[0:total, :].reshape(total // PR, PR, TL).astype(BF16)
     for d in far:
         pltpu.make_async_remote_copy(
             send2, got2.at[z], s2, r2, device_id=((z + d) % NZ, col), device_id_type=MESH
@@ -375,11 +398,12 @@
             pltpu.VMEM((NP, PR, TL), BF16),
             pltpu.VMEM((NP, PR, TL), BF16),
             pltpu.VMEM((-(-total // TR) * TR, NP * PR), BF16),
-            pltpu.VMEM((total, TL), BF16),
-            pltpu.VMEM((NZ, total, TL), BF16),
+            pltpu.VMEM((total // PR, PR, TL), BF16),
+            pltpu.VMEM((NZ, total // PR, PR, TL), BF16),
             pltpu.VMEM((3 * SLOTS, NZ * total), BF16),
             pltpu.VMEM((3 * SLOTS, TL), BF16),
             dma((5,)), dma, dma, dma, dma, dma, dma((NCH - 1,)), dma, dma,
+            pltpu.SemaphoreType.REGULAR, pltpu.SemaphoreType.REGULAR,
         ],
         compiler_params=pltpu.CompilerParams(
             collective_id=0 if fast else 1, has_side_effects=True, vmem_limit_bytes=24 * 2**20

time: 43.9 us -> 43.3 us (0.986)
  Pallas kernels: 41.8 us -> 41.2 us
    pallas_call x1, Pallas kernels: 37.4 us -> 36.8 us  [run_exchange(): pl.pallas_call(functools.partial(exchange, cap, step, total, fast), name=...]
where the time goes in v5:
time: 43.3 us; the launch traced here: 43.1 us
  Pallas kernels  41.2 us (95%)
  between operations  1.89 us (4%)
    pallas_call x1, Pallas kernels, run_exchange(): pl.pallas_call(functools.partial(exchange, cap, step, total, fast), name=...  36.8 us
    pallas_call x1, Pallas kernels, run_compute(): pl.pallas_call(compute, name='compute', out_shape=(jax.ShapeDtypeStruct((...  4.35 us

profile of v5, /device:TPU:1, one launch (start us, length us, event | category | flops | bytes accessed | tf_op | source)
XLA Modules:
  0.0 43.1 jit_solution(14897568032984715704)
XLA Ops:
  1.3 36.8 %exchange.1 = (bf16[128,384]{1,0:T(8,128)(2,1)S(1)}, bf16[2,16,96,128]{3,2,1,0:T(8,128)(2,1)S(1)}, bf16[960,960]{1,0:T(8,128)(2,1)S(1)}, bf16[960,960]{1,0:T(8,128)(2,1)S(1)}, s32[1]{0:T(128)}) custom-call(s32[1024]{0:T(1024)} %refs_0_.1, s32[1]{0:T(128)S(6)} %copy.15.refs_1_, bf16[60,2,190]{2,1,0:T(2,128)(2,1)} %bitcast.2, bf16[2,190]{1,0:T(2,128)(2,1)} %refs_3_.1, ...), custom_call_target="tpu_custom_call" | custom-call | tf_op jit(solution)/shard_map/exchange/pallas_call | solution.py:384
  38.7 0.0 copy-start
  38.7 0.0 copy-start.1
  38.7 0.0 copy-start.2
  38.7 0.0 copy-start.3
  38.7 4.4 %compute.3 = (bf16[120,960]{1,0:T(8,128)(2,1)}, bf16[120,960]{1,0:T(8,128)(2,1)}) custom-call(bf16[128,384]{1,0:T(8,128)(2,1)S(1)} %get-tuple-element.37.own_ref, bf16[2,16,96,128]{3,2,1,0:T(8,128)(2,1)S(1)} %get-tuple-element.38.all_ref, bf16[960,960]{1,0:T(8,128)(2,1)S(1)} %get-tuple-element.35.inv_ref, bf16[960,960]{1,0:T(8,128)(2,1)S(1)} %get-tuple-element.36.perm_ref), custom_call_target="tpu_custom_call" | custom-call | tf_op jit(solution)/shard_map/compute/pallas_call | solution.py:416
  43.1 0.0 copy-done
  43.1 0.0 copy-done.1
  43.1 0.0 copy-done.2
  43.1 0.0 copy-done.3
  (1 shorter events, 0.0 us)
Async XLA Ops:
  38.7 4.4 %copy-start = (bf16[960,960]{1,0:T(8,128)(2,1)S(1)}, bf16[960,960]{1,0:T(8,128)(2,1)}, u32[]{:S(2)}) copy-start(bf16[960,960]{1,0:T(8,128)(2,1)} %refs_4_.1) | copy-start | bytes 5529604
  38.7 4.4 %copy-start.1 = (bf16[2,60,190]{2,0,1:T(2,128)(2,1)S(1)}, bf16[2,60,190]{2,0,1:T(2,128)(2,1)}, u32[]{:S(2)}) copy-start(bf16[2,60,190]{2,0,1:T(2,128)(2,1)} %param.7) | copy-start | bytes 136804
  38.7 4.4 %copy-start.2 = (s32[1024]{0:T(1024)S(1)}, s32[1024]{0:T(1024)}, u32[]{:S(2)}) copy-start(s32[1024]{0:T(1024)} %refs_0_.1) | copy-start | bytes 12292
  38.7 4.4 %copy-start.3 = (bf16[2,190]{1,0:T(2,128)(2,1)S(1)}, bf16[2,190]{1,0:T(2,128)(2,1)}, u32[]{:S(2)}) copy-start(bf16[2,190]{1,0:T(2,128)(2,1)} %refs_3_.1) | copy-start | bytes 2284

commit v6 on v5

--- a/solution.py
+++ b/solution.py
@@ -74,7 +74,7 @@
         send1[q] = stage[q].astype(BF16)
 
 
-def choices(order, panel, z, cap, step, total, one1, one2, over_ref, fast):
+def choices(order, panel, z, cap, step, one1, one2, flag, fast):
     base = panel[0] * TR
     lane = iota((8, TL), 1)
     sub = iota((8, TL), 0)
@@ -96,8 +96,8 @@
     same = plane_col == plane_row
     before = jnp.logical_and(same, slot_row < slot_col)
     rank_col = jnp.sum(jnp.where(before, 1.0, 0.0), axis=1, keepdims=True)
-    if over_ref is not None:
-        over_ref[0] = jnp.where(jnp.max(rank_col) >= cap, 1, 0)
+    if fast:
+        flag[0] = jnp.where(jnp.max(rank_col) >= cap, 1, 0)
     rank_col = jnp.broadcast_to(rank_col, (SLOTS, TL)).astype(jnp.int32)
     place = rank_col if fast else slot_col
     here = plane_col == z
@@ -110,9 +110,8 @@
         for t in range(NP * PR // TL):
             find.append(jnp.logical_and(at == slot_row + TL * t, here))
         finds.append(onehot(jnp.concatenate(find, axis=1)))
-        goal = plane_col * total + kind * step + place
-        take = [goal == slot_row + TL * t for t in range(NZ * total // TL)]
-        one2[kind * SLOTS : kind * SLOTS + SLOTS, :] = onehot(jnp.concatenate(take, axis=1))
+    goal = plane_col * step + place
+    one2[...] = onehot(jnp.concatenate([goal == slot_row + TL * t for t in range(NZ * step // TL)], axis=1))
     finds = jnp.concatenate(finds, axis=0)
     if fast:
         after = jnp.logical_and(same, slot_col < slot_row)
@@ -138,7 +137,7 @@
         own_ref, all_ref = refs[5:7]
         inv_out = perm_out = over_ref = None
         rest = refs[7:]
-    (order, panel, jac, desc, inv, blk, stage, send1, got1, one1, send2, got2, one2, mine, ins,
+    (flag, order, panel, jac, desc, inv, blk, stage, send1, got1, one1, send2, got2, one2, mine, ins,
      s1, r1, s2, r2, s4, r4, s5, r5, plane, line) = rest
     z = lax.axis_index("row")
     col = lax.axis_index("col")
@@ -189,8 +188,10 @@
     got1[col] = send1[col]
     loads[2].wait()
     loads[3].wait()
-    choices(order, panel, z, cap, step, total, one1, one2, over_ref, fast)
-    if fast:
+    choices(order, panel, z, cap, step, one1, one2, flag, fast)
+    if fast:
+        told = pltpu.make_async_copy(flag, over_ref, ins.at[5])
+        told.start()
         at = iota((PCOLS, PCOLS), 1)
         perm_out[...] = onehot(iota((PCOLS, PCOLS), 0) == (at % TR) * NC + at // TR)
         loads[4].wait()
@@ -207,12 +208,14 @@
     pltpu.make_async_copy(got1.at[0 : NP - 1], got1.at[0 : NP - 1], r1).wait()
 
     held = got1[...].astype(F32).reshape(NP * PR, TL).astype(BF16)
-    send2[...] = dot(one1[...], held, NN)[0:total, :].reshape(total // PR, PR, TL).astype(BF16)
-    for d in far:
-        pltpu.make_async_remote_copy(
-            send2, got2.at[z], s2, r2, device_id=((z + d) % NZ, col), device_id_type=MESH
-        ).start()
-    got2[z] = send2[...]
+    send2[...] = dot(one1[...], held, NN)[0:total, :].reshape(3, step // PR, PR, TL).astype(BF16)
+    for kind in range(3):
+        for d in far:
+            pltpu.make_async_remote_copy(
+                send2.at[kind], got2.at[kind, z], s2, r2.at[kind],
+                device_id=((z + d) % NZ, col), device_id_type=MESH,
+            ).start()
+        got2[kind, z] = send2[kind]
     if fast:
 
         @pl.loop(0, 3)
@@ -220,34 +223,42 @@
             rows = pl.ds(pl.multiple_of(g * 320, 320), 320)
             inv_out[rows, :] = dot(inv[rows, :], perm_out[...], NN).astype(BF16)
 
-    pltpu.make_async_copy(got2.at[0 : NZ - 1], got2.at[0 : NZ - 1], r2).wait()
-    held = got2[...].astype(F32).reshape(NZ * total, TL).astype(BF16)
-    mine[...] = dot(one2[...], held, NN).astype(BF16)
-
     steps = steps[:-1]
-    for n, (dx, dy) in enumerate(steps):
-        to = (((x + dx) % 4) * 4 + (y + dy) % 4) * 2 + core
+    for kind in range(3):
+        part = got2.at[kind, 0 : NZ - 1]
+        pltpu.make_async_copy(part, part, r2.at[kind]).wait()
+        held = got2[kind].astype(F32).reshape(NZ * step, TL).astype(BF16)
+        rows = pl.ds(kind * SLOTS, SLOTS)
+        mine[rows, :] = dot(one2[...], held, NN).astype(BF16)
+        for n, (dx, dy) in enumerate(steps):
+            to = (((x + dx) % 4) * 4 + (y + dy) % 4) * 2 + core
+            pltpu.make_async_remote_copy(
+                mine.at[rows], all_ref.at[core, chip, rows], s4, r4.at[kind, n],
+                device_id=(z, to), device_id_type=MESH,
+            ).start()
         pltpu.make_async_remote_copy(
-            mine, all_ref.at[core, chip], s4, r4.at[n], device_id=(z, to), device_id_type=MESH
+            mine.at[rows], all_ref.at[core, chip, rows], s5, r5, device_id=(z, sib), device_id_type=MESH
         ).start()
-    pltpu.make_async_remote_copy(
-        mine, all_ref.at[core, chip], s5, r5, device_id=(z, sib), device_id_type=MESH
-    ).start()
     all_ref[core, chip] = mine[...]
-    for n, (dx, dy) in reversed(list(enumerate(steps))):
-        source = ((x + 4 - dx) % 4) * 4 + (y + 4 - dy) % 4
-        landed = all_ref.at[core, source]
-        pltpu.make_async_copy(landed, landed, r4.at[n]).wait()
-        pltpu.make_async_remote_copy(
-            landed, landed, s5, r5, device_id=(z, sib), device_id_type=MESH
-        ).start()
+    for kind in range(3):
+        rows = pl.ds(kind * SLOTS, SLOTS)
+        for n, (dx, dy) in reversed(list(enumerate(steps))):
+            source = ((x + 4 - dx) % 4) * 4 + (y + 4 - dy) % 4
+            landed = all_ref.at[core, source, rows]
+            pltpu.make_async_copy(landed, landed, r4.at[kind, n]).wait()
+            pltpu.make_async_remote_copy(
+                landed, landed, s5, r5, device_id=(z, sib), device_id_type=MESH
+            ).start()
     other = all_ref.at[1 - core]
     pltpu.make_async_copy(other, other, r5).wait()
 
     pltpu.make_async_copy(got1.at[0 : NP - 1], got1.at[0 : NP - 1], s1).wait()
-    pltpu.make_async_copy(got2.at[0 : NZ - 1], got2.at[0 : NZ - 1], s2).wait()
+    every = got2.at[0:3, 0 : NZ - 1]
+    pltpu.make_async_copy(every, every, s2).wait()
     pltpu.make_async_copy(all_ref.at[0, 0:15], all_ref.at[0, 0:15], s4).wait()
     pltpu.make_async_copy(other, other, s5).wait()
+    if fast:
+        told.wait()
 
 
 def compute(own_ref, all_ref, inv_ref, perm_ref, factor_ref, next_ref, rhs, lhs, lhs2, dexp, cross, outs):
@@ -379,7 +390,7 @@
     specs = (VM, VM)
     if fast:
         outs += (square, square, jax.ShapeDtypeStruct((1,), jnp.int32))
-        specs += (VM, VM, pl.BlockSpec(memory_space=pltpu.SMEM))
+        specs += (VM, VM, HBM)
     dma = pltpu.SemaphoreType.DMA
     return pl.pallas_call(
         functools.partial(exchange, cap, step, total, fast),
@@ -388,6 +399,7 @@
         in_specs=[HBM] * 5,
         out_specs=specs,
         scratch_shapes=[
+            pltpu.SMEM((1,), jnp.int32),
             pltpu.SMEM((NZ * 2 * NP,), jnp.int32),
             pltpu.SMEM((1,), jnp.int32),
             pltpu.VMEM(jac.shape, BF16),
@@ -398,11 +410,11 @@
             pltpu.VMEM((NP, PR, TL), BF16),
             pltpu.VMEM((NP, PR, TL), BF16),
             pltpu.VMEM((-(-total // TR) * TR, NP * PR), BF16),
-            pltpu.VMEM((total // PR, PR, TL), BF16),
-            pltpu.VMEM((NZ, total // PR, PR, TL), BF16),
-            pltpu.VMEM((3 * SLOTS, NZ * total), BF16),
+            pltpu.VMEM((3, step // PR, PR, TL), BF16),
+            pltpu.VMEM((3, NZ, step // PR, PR, TL), BF16),
+            pltpu.VMEM((SLOTS, NZ * step), BF16),
             pltpu.VMEM((3 * SLOTS, TL), BF16),
-            dma((5,)), dma, dma, dma, dma, dma, dma((NCH - 1,)), dma, dma,
+            dma((6,)), dma, dma, dma, dma((3,)), dma, dma((3, NCH - 1)), dma, dma,
             pltpu.SemaphoreType.REGULAR, pltpu.SemaphoreType.REGULAR,
         ],
         compiler_params=pltpu.CompilerParams(

time: 43.3 us -> 43.6 us (level)
  no operation moved by 1% of the time
where the time goes in v6:
time: 43.6 us; the launch traced here: 43.4 us
  Pallas kernels  41.5 us (95%)
  between operations  1.89 us (4%)
    pallas_call x1, Pallas kernels, run_exchange(): pl.pallas_call(functools.partial(exchange, cap, step, total, fast), name=...  37.1 us
    pallas_call x1, Pallas kernels, run_compute(): pl.pallas_call(compute, name='compute', out_shape=(jax.ShapeDtypeStruct((...  4.36 us

profile of v6, /device:TPU:1, one launch (start us, length us, event | category | flops | bytes accessed | tf_op | source)
XLA Modules:
  0.0 43.4 jit_solution(1479540413504649101)
XLA Ops:
  1.3 37.1 %exchange.1 = (bf16[128,384]{1,0:T(8,128)(2,1)S(1)}, bf16[2,16,96,128]{3,2,1,0:T(8,128)(2,1)S(1)}, bf16[960,960]{1,0:T(8,128)(2,1)S(1)}, bf16[960,960]{1,0:T(8,128)(2,1)S(1)}, s32[1]{0:T(128)}) custom-call(s32[1024]{0:T(1024)} %refs_0_.1, s32[1]{0:T(128)S(6)} %copy.15.refs_1_, bf16[60,2,190]{2,1,0:T(2,128)(2,1)} %bitcast.2, bf16[2,190]{1,0:T(2,128)(2,1)} %refs_3_.1, ...), custom_call_target="tpu_custom_call" | custom-call | tf_op jit(solution)/shard_map/exchange/pallas_call | solution.py:395
  39.0 0.0 copy-start
  39.0 0.0 copy-start.1
  39.0 0.0 copy-start.2
  39.0 0.0 copy-start.3
  39.0 4.4 %compute.3 = (bf16[120,960]{1,0:T(8,128)(2,1)}, bf16[120,960]{1,0:T(8,128)(2,1)}) custom-call(bf16[128,384]{1,0:T(8,128)(2,1)S(1)} %get-tuple-element.37.own_ref, bf16[2,16,96,128]{3,2,1,0:T(8,128)(2,1)S(1)} %get-tuple-element.38.all_ref, bf16[960,960]{1,0:T(8,128)(2,1)S(1)} %get-tuple-element.35.inv_ref, bf16[960,960]{1,0:T(8,128)(2,1)S(1)} %get-tuple-element.36.perm_ref), custom_call_target="tpu_custom_call" | custom-call | tf_op jit(solution)/shard_map/compute/pallas_call | solution.py:428
  43.4 0.0 copy-done
  43.4 0.0 copy-done.1
  43.4 0.0 copy-done.2
  43.4 0.0 copy-done.3
  (1 shorter events, 0.0 us)
Async XLA Ops:
  39.0 4.4 %copy-start = (bf16[960,960]{1,0:T(8,128)(2,1)S(1)}, bf16[960,960]{1,0:T(8,128)(2,1)}, u32[]{:S(2)}) copy-start(bf16[960,960]{1,0:T(8,128)(2,1)} %refs_4_.1) | copy-start | bytes 5529604
  39.0 4.4 %copy-start.1 = (bf16[2,60,190]{2,0,1:T(2,128)(2,1)S(1)}, bf16[2,60,190]{2,0,1:T(2,128)(2,1)}, u32[]{:S(2)}) copy-start(bf16[2,60,190]{2,0,1:T(2,128)(2,1)} %param.7) | copy-start | bytes 136804
  39.0 4.4 %copy-start.2 = (s32[1024]{0:T(1024)S(1)}, s32[1024]{0:T(1024)}, u32[]{:S(2)}) copy-start(s32[1024]{0:T(1024)} %refs_0_.1) | copy-start | bytes 12292
  39.0 4.4 %copy-start.3 = (bf16[2,190]{1,0:T(2,128)(2,1)S(1)}, bf16[2,190]{1,0:T(2,128)(2,1)}, u32[]{:S(2)}) copy-start(bf16[2,190]{1,0:T(2,128)(2,1)} %refs_3_.1) | copy-start | bytes 2284

commit v7 on v6

--- a/solution.py
+++ b/solution.py
@@ -209,12 +209,13 @@
 
     held = got1[...].astype(F32).reshape(NP * PR, TL).astype(BF16)
     send2[...] = dot(one1[...], held, NN)[0:total, :].reshape(3, step // PR, PR, TL).astype(BF16)
-    for kind in range(3):
-        for d in far:
+    for d in far:
+        for kind in range(3):
             pltpu.make_async_remote_copy(
                 send2.at[kind], got2.at[kind, z], s2, r2.at[kind],
                 device_id=((z + d) % NZ, col), device_id_type=MESH,
             ).start()
+    for kind in range(3):
         got2[kind, z] = send2[kind]
     if fast:
 

time: 43.6 us -> 43.1 us (0.989)
  Pallas kernels: 41.5 us -> 41 us
    pallas_call x1, Pallas kernels: 37.1 us -> 36.6 us  [run_exchange(): pl.pallas_call(functools.partial(exchange, cap, step, total, fast), name=...]
where the time goes in v7:
time: 43.1 us; the launch traced here: 42.9 us
  Pallas kernels  41 us (95%)
  between operations  1.89 us (4%)
    pallas_call x1, Pallas kernels, run_exchange(): pl.pallas_call(functools.partial(exchange, cap, step, total, fast), name=...  36.6 us
    pallas_call x1, Pallas kernels, run_compute(): pl.pallas_call(compute, name='compute', out_shape=(jax.ShapeDtypeStruct((...  4.36 us

profile of v7, /device:TPU:1, one launch (start us, length us, event | category | flops | bytes accessed | tf_op | source)
XLA Modules:
  0.0 42.9 jit_solution(7435910039955420253)
XLA Ops:
  1.3 36.6 %exchange.1 = (bf16[128,384]{1,0:T(8,128)(2,1)S(1)}, bf16[2,16,96,128]{3,2,1,0:T(8,128)(2,1)S(1)}, bf16[960,960]{1,0:T(8,128)(2,1)S(1)}, bf16[960,960]{1,0:T(8,128)(2,1)S(1)}, s32[1]{0:T(128)}) custom-call(s32[1024]{0:T(1024)} %refs_0_.1, s32[1]{0:T(128)S(6)} %copy.15.refs_1_, bf16[60,2,190]{2,1,0:T(2,128)(2,1)} %bitcast.2, bf16[2,190]{1,0:T(2,128)(2,1)} %refs_3_.1, ...), custom_call_target="tpu_custom_call" | custom-call | tf_op jit(solution)/shard_map/exchange/pallas_call | solution.py:396
  38.5 0.0 copy-start
  38.5 0.0 copy-start.1
  38.5 0.0 copy-start.2
  38.5 0.0 copy-start.3
  38.5 4.4 %compute.3 = (bf16[120,960]{1,0:T(8,128)(2,1)}, bf16[120,960]{1,0:T(8,128)(2,1)}) custom-call(bf16[128,384]{1,0:T(8,128)(2,1)S(1)} %get-tuple-element.37.own_ref, bf16[2,16,96,128]{3,2,1,0:T(8,128)(2,1)S(1)} %get-tuple-element.38.all_ref, bf16[960,960]{1,0:T(8,128)(2,1)S(1)} %get-tuple-element.35.inv_ref, bf16[960,960]{1,0:T(8,128)(2,1)S(1)} %get-tuple-element.36.perm_ref), custom_call_target="tpu_custom_call" | custom-call | tf_op jit(solution)/shard_map/compute/pallas_call | solution.py:429
  42.9 0.0 copy-done
  42.9 0.0 copy-done.1
  42.9 0.0 copy-done.2
  42.9 0.0 copy-done.3
  (1 shorter events, 0.0 us)
Async XLA Ops:
  38.5 4.4 %copy-start = (bf16[960,960]{1,0:T(8,128)(2,1)S(1)}, bf16[960,960]{1,0:T(8,128)(2,1)}, u32[]{:S(2)}) copy-start(bf16[960,960]{1,0:T(8,128)(2,1)} %refs_4_.1) | copy-start | bytes 5529604
  38.5 4.4 %copy-start.1 = (bf16[2,60,190]{2,0,1:T(2,128)(2,1)S(1)}, bf16[2,60,190]{2,0,1:T(2,128)(2,1)}, u32[]{:S(2)}) copy-start(bf16[2,60,190]{2,0,1:T(2,128)(2,1)} %param.7) | copy-start | bytes 136804
  38.5 4.4 %copy-start.2 = (s32[1024]{0:T(1024)S(1)}, s32[1024]{0:T(1024)}, u32[]{:S(2)}) copy-start(s32[1024]{0:T(1024)} %refs_0_.1) | copy-start | bytes 12292
  38.5 4.4 %copy-start.3 = (bf16[2,190]{1,0:T(2,128)(2,1)S(1)}, bf16[2,190]{1,0:T(2,128)(2,1)}, u32[]{:S(2)}) copy-start(bf16[2,190]{1,0:T(2,128)(2,1)} %refs_3_.1) | copy-start | bytes 2284
